TPU v7x, 512 devices: a whole 4x8x8 slice. The times are simulated.
512 devices in a mesh: dp: 4 (over x), ctx: 16 (over y_lo, z), vocab: 8 (over y_hi, core).
Axes of the slice: x: 4, y: 8 (y_hi: 4, y_lo: 2; y = y_hi * 2 + y_lo), z: 8, core: 2. Of those that a mesh axis runs over, the one named last changes fastest.
Arguments:
- hidden: bfloat16 [32768, 5376], P(('dp', 'ctx'), 'vocab'), may hold values from -60 to 60
- embedding: bfloat16 [1024, 5376], P('vocab', ('dp', 'ctx')), may hold values from -1 to 1, as said below
- targets: int32 [32768], P(('dp', 'ctx')), may hold values from 0 to 1023, as said below
- pattern: int32 [256, 8], P(('dp', 'ctx'), 'vocab'), may hold values from 0 to 1, as said below
- loss_grad: float32 [32768], P(('dp', 'ctx')), may hold values from 0.3 to 3
Outputs:
- loss: float32 [32768], P(('dp', 'ctx'))
- hidden_grad: bfloat16 [32768, 5376], P(('dp', 'ctx'), 'vocab')
- embedding_grad: float32 [1024, 5376], P('vocab', ('dp', 'ctx'))
Inputs may be any that keep to these rules, and one draw needn't show every extreme that they name: `targets`: each token's target lies in a vocabulary block that pattern marks for the token's block. `pattern`: every token block has at least one marked vocabulary block. `embedding`: every row has unit Euclidean length before rounding.
All inputs are finite; a program needn't handle non-finite values.
Results may differ from a plain program's by a relative error of at most 0.005.
Values may be sent and summed in bfloat16 or wider, within the bound.
A program may use at most 64 MiB of HBM per device.

v0:
```python
from functools import partial

import jax
import jax.numpy as jnp
from jax import lax
from jax.sharding import PartitionSpec as P

TILE = 128


def score_tile(features, weights):
    return lax.dot_general(
        features, weights, (((1,), (1,)), ((), ())), preferred_element_type=jnp.float32
    )


def grad_tile(grads, features):
    return lax.dot_general(
        grads, features, (((0,), (0,)), ((), ())), preferred_element_type=jnp.float32
    )


def empty_tile(shape):
    return jnp.zeros(shape, jnp.float32)


def on_device(hidden, embedding, targets, pattern, loss_grad):
    tok_rows = hidden.shape[0]
    voc_rows = embedding.shape[0]
    table = lax.all_gather(embedding, ("dp", "ctx"), axis=1, tiled=True)
    whole = lax.all_gather(hidden, "vocab", axis=1, tiled=True)
    width = whole.shape[1]
    first_col = lax.axis_index("vocab") * voc_rows
    columns = first_col + lax.iota(jnp.int32, voc_rows)
    target_hit = targets[:, None] == columns[None, :]
    live = jnp.repeat(jnp.repeat(pattern > 0, TILE, axis=0), TILE, axis=1)
    token_blocks = tok_rows // TILE
    strips = []
    for row_block in range(token_blocks):
        feats = whole[row_block * TILE : (row_block + 1) * TILE]
        col_block = 0
        pieces = lax.cond(
            pattern[row_block, col_block] > 0,
            partial(score_tile, feats, table),
            partial(empty_tile, (TILE, TILE)),
        )
        strips.append(pieces)
    logits = jnp.concatenate(strips, axis=0)
    local_max = jnp.max(jnp.where(live, logits, jnp.float32(-1e30)), axis=1)
    target_part = jnp.sum(jnp.where(target_hit, logits, jnp.float32(0.0)), axis=1)
    peak = lax.pmax(local_max, "vocab")
    local_sum = jnp.sum(jnp.where(live, jnp.exp(logits - peak[:, None]), jnp.float32(0.0)), axis=1)
    total, target_logit = lax.psum((local_sum, target_part), "vocab")
    lse = peak + jnp.log(total)
    loss = lse - target_logit
    probs = jnp.where(live, jnp.exp(logits - lse[:, None]), jnp.float32(0.0))
    logit_grad = (loss_grad[:, None] * (probs - target_hit.astype(jnp.float32))).astype(
        jnp.bfloat16
    )
    col_block = 0
    running = jnp.zeros((TILE, width), jnp.float32)
    for row_block in range(token_blocks):
        feats = whole[row_block * TILE : (row_block + 1) * TILE]
        grads = logit_grad[
            row_block * TILE : (row_block + 1) * TILE, col_block * TILE : (col_block + 1) * TILE
        ]
        running = running + lax.cond(
            pattern[row_block, col_block] > 0,
            partial(grad_tile, grads, feats),
            partial(empty_tile, (TILE, width)),
        )
    embedding_grad = lax.psum_scatter(running, ("dp", "ctx"), scatter_dimension=1, tiled=True)
    table_cols = lax.all_to_all(table, "vocab", split_axis=1, concat_axis=0, tiled=True)
    hidden_sum = jnp.dot(
        lax.all_gather(logit_grad, "vocab", axis=1, tiled=True),
        table_cols,
        preferred_element_type=jnp.float32,
    )
    return (loss, hidden_sum.astype(jnp.bfloat16), embedding_grad)


def solution(mesh):
    return jax.shard_map(
        on_device,
        mesh=mesh,
        in_specs=(
            P(("dp", "ctx"), "vocab"),
            P("vocab", ("dp", "ctx")),
            P(("dp", "ctx")),
            P(("dp", "ctx"), "vocab"),
            P(("dp", "ctx")),
        ),
        out_specs=(P(("dp", "ctx")), P(("dp", "ctx"), "vocab"), P("vocab", ("dp", "ctx"))),
        check_vma=False,
    )
```

profile of v0, /device:TPU:4, one launch (start us, length us, event | category | flops | bytes accessed | tf_op | source)
XLA Modules:
  0.0 681.6 jit_solution(7531866524642247518)
XLA Ops:
  7.2 0.0 all-gather.9.cloned.1.call-start
  7.2 0.7 all-gather.9.cloned.1.call-update
  7.9 0.0 all-gather.5.cloned.1.call-start
  7.9 0.7 all-gather.5.cloned.1.call-update
  8.7 1.5 fusion.21
  12.7 0.7 compare_bitcast_fusion
  13.4 0.1 broadcast_bitcast_fusion
  13.5 268.7 %all-gather.9.cloned.1.call-done = bf16[64,84,128]{2,1,0:T(8,128)(2,1)} async-done(((bf16[1,84,128]{2,1,0:T(8,128)(2,1)}), bf16[64,84,128]{2,1,0:T(8,128)(2,1)}) %all-gather.9.cloned.1.call-update) | async-done | bytes 1376272 | tf_op jit(solution)/shard_map/all_gather | solution.py:30
  282.2 3.2 reshape.47
  285.4 5.8 all-to-all-start
  291.2 0.0 all-gather.7.cloned.1.call-start
  291.3 88.8 %all-gather.5.cloned.1.call-done = bf16[512,5376]{0,1:T(8,128)(2,1)} async-done(((bf16[512,672]{0,1:T(8,128)(2,1)}), bf16[512,5376]{0,1:T(8,128)(2,1)}) %all-gather.5.cloned.1.call-update) | async-done | bytes 5505040 | tf_op jit(solution)/shard_map/all_gather | solution.py:31
  380.1 4.6 fusion.20
  384.7 2.3 conditional.11
  384.7 2.3 fusion.25
  387.0 2.3 conditional.10
  387.0 2.3 fusion.24
  389.3 1.9 conditional.9
  389.4 1.9 fusion.23
  391.3 0.0 copy-start.3
  391.3 0.0 copy-start.4
  391.3 1.9 conditional.8
  391.3 1.9 fusion.22
  393.2 0.2 select_reduce_fusion.1
  393.5 14.2 %pmax.7 = f32[512]{0:T(512)S(1)} all-reduce(f32[512]{0:T(512)S(1)} %select_reduce_fusion.1), channel_id=1, replica_groups=mesh['dp'=4,'ctx'=16,'vocab'=8] {'vocab'}, use_global_device_ids=true, to_apply=%region_9.10 | all-reduce | flops 512 | bytes 4096 | tf_op jit(solution)/shard_map/pmax | solution.py:51
  407.7 0.4 fusion.15
  408.1 14.2 %all-reduce.2 = (f32[512]{0:T(512)S(1)}, f32[512]{0:T(512)S(1)}) all-reduce(f32[512]{0:T(512)S(1)} %get-tuple-element.108, f32[512]{0:T(512)S(1)} %get-tuple-element.107), channel_id=1, replica_groups=mesh['dp'=4,'ctx'=16,'vocab'=8] {'vocab'}, use_global_device_ids=true, to_apply=%region_11.12 | all-reduce | flops 1024 | bytes 8192 | tf_op jit(solution)/shard_map/psum | solution.py:53
  422.3 0.6 fusion.19
  422.9 1.0 fusion.18
  423.9 0.0 all-gather.7.cloned.1.call-update
  423.9 1.9 conditional.15
  424.0 1.8 fusion.7
  425.8 1.5 copy-done
  427.3 1.8 conditional.14
  427.3 1.8 fusion.5
  429.2 1.5 copy-done.1
  430.7 1.3 conditional.12
  430.7 1.3 fusion.1
  432.0 1.5 copy-done.2
  433.5 2.9 conditional.13
  433.5 2.9 fusion.3
  436.4 6.3 add_add_fusion
  442.8 157.8 %fusion = f32[128,96]{0,1:T(8,128)S(1)} fusion(f32[128,5376]{0,1:T(8,128)} %add_add_fusion), kind=kCustom, calls=%all-reduce-scatter | all-reduce-scatter fusion | flops 786433 | bytes 2803712
  600.6 1.9 collective-permute-start.6
  602.5 8.9 %collective-permute-start.5 = (f32[128,96]{0,1:T(8,128)S(1)}, f32[128,96]{0,1:T(8,128)S(1)}, u32[]{:S(2)}, u32[]{:S(2)}) collective-permute-start(f32[128,96]{0,1:T(8,128)S(1)} %fusion), channel_id=1, source_target_pairs={{0,48},{8,56},{16,64},{24,72},{32,80},{40,88},{48,96},{56,104},{64... | collective-permute-start | bytes 147464
  611.4 14.7 %collective-permute-start.7 = (f32[128,84]{0,1:T(8,128)S(1)}, f32[128,84]{0,1:T(8,128)S(1)}, u32[]{:S(2)}, u32[]{:S(2)}) collective-permute-start(f32[128,84]{0,1:T(8,128)S(1)} %slice.60), channel_id=1, source_target_pairs={{0,64},{8,72},{16,80},{24,88},{32,96},{40,104},{48,112},{56,120},{... | collective-permute-start | bytes 129032
  626.1 15.4 %collective-permute-start.4 = (f32[128,96]{0,1:T(8,128)S(1)}, f32[128,96]{0,1:T(8,128)S(1)}, u32[]{:S(2)}, u32[]{:S(2)}) collective-permute-start(f32[128,96]{0,1:T(8,128)S(1)} %fusion), channel_id=1, source_target_pairs={{0,40},{8,48},{16,56},{24,64},{32,72},{40,80},{48,88},{56,96},{64,... | collective-permute-start | bytes 147464
  641.5 10.8 %collective-permute-start.3 = (f32[128,96]{0,1:T(8,128)S(1)}, f32[128,96]{0,1:T(8,128)S(1)}, u32[]{:S(2)}, u32[]{:S(2)}) collective-permute-start(f32[128,96]{0,1:T(8,128)S(1)} %fusion), channel_id=1, source_target_pairs={{0,32},{8,40},{16,48},{24,56},{32,64},{40,72},{48,80},{56,88},{64,... | collective-permute-start | bytes 147464
  652.4 0.0 collective-permute-done.7
  652.4 1.9 collective-permute-start.2
  654.3 0.0 collective-permute-done.6
  654.3 6.3 collective-permute-start.1
  660.6 0.0 collective-permute-done.5
  660.6 3.4 collective-permute-start
  664.0 1.3 dynamic-slice.4
  665.9 0.0 collective-permute-done.4
  665.9 0.0 collective-permute-done.3
  665.9 0.0 collective-permute-done.2
  666.0 2.1 collective-permute-done.1
  668.0 1.6 collective-permute-done
  669.6 1.4 concatenate.4
  671.0 0.6 constant_dynamic-slice_fusion
  671.7 0.0 all-to-all-done
  671.7 3.4 fusion.12
  (8 shorter events, 0.0 us)
Async XLA Ops:
  7.2 275.0 %all-gather.9.cloned.1.call-start = ((), (), s32[]{:S(2)}) async-start(), calls=%async_computation.3 | async-start | bytes 1464320 | tf_op jit(solution)/shard_map/all_gather | solution.py:30
  7.9 372.2 %all-gather.5.cloned.1.call-start = ((), (), s32[]{:S(2)}) async-start(), calls=%async_computation.1 | async-start | bytes 6193152 | tf_op jit(solution)/shard_map/all_gather | solution.py:31
  285.4 386.3 %all-to-all-start = ((bf16[128,8,672]{0,2,1:T(8,128)(2,1)}), bf16[128,8,672]{0,2,1:T(8,128)(2,1)}, u32[]{:S(2)}, u32[]{:S(2)}) async-start(bf16[128,8,672]{0,2,1:T(8,128)(2,1)} %bitcast.9), calls=%async_computation | async-start | bytes 2752512 | tf_op jit(solution)/shard_map/all_to_all | solution.py:73
  291.2 380.4 %all-gather.7.cloned.1.call-start = ((), (), s32[]{:S(2)}) async-start(), calls=%async_computation.2 | async-start | bytes 1179648 | tf_op jit(solution)/shard_map/all_gather | solution.py:75
  391.3 16.4 %copy-start.3 = (s32[512]{0:T(512)S(1)}, s32[512]{0:T(512)}, u32[]{:S(2)}) copy-start(s32[512]{0:T(512)} %param.23) | copy-start | bytes 6148
  391.3 31.6 %copy-start.4 = (f32[512]{0:T(512)S(1)}, f32[512]{0:T(512)}, u32[]{:S(2)}) copy-start(f32[512]{0:T(512)} %param.25) | copy-start | bytes 6148
  425.8 1.5 copy-start
  429.2 1.6 copy-start.1
  432.0 1.6 copy-start.2
  600.6 53.7 %collective-permute-start.6 = (f32[128,96]{0,1:T(8,128)S(1)}, f32[128,96]{0,1:T(8,128)S(1)}, u32[]{:S(2)}, u32[]{:S(2)}) collective-permute-start(f32[128,96]{0,1:T(8,128)S(1)} %fusion), channel_id=1, source_target_pairs={{0,56},{8,64},{16,72},{24,80},{32,88},{40,96},{48,104},{56,112},{6... | collective-permute-start | bytes 147464
  602.5 58.1 %collective-permute-start.5 = (f32[128,96]{0,1:T(8,128)S(1)}, f32[128,96]{0,1:T(8,128)S(1)}, u32[]{:S(2)}, u32[]{:S(2)}) collective-permute-start(f32[128,96]{0,1:T(8,128)S(1)} %fusion), channel_id=1, source_target_pairs={{0,48},{8,56},{16,64},{24,72},{32,80},{40,88},{48,96},{56,104},{64... | collective-permute-start | bytes 147464
  611.4 41.0 %collective-permute-start.7 = (f32[128,84]{0,1:T(8,128)S(1)}, f32[128,84]{0,1:T(8,128)S(1)}, u32[]{:S(2)}, u32[]{:S(2)}) collective-permute-start(f32[128,84]{0,1:T(8,128)S(1)} %slice.60), channel_id=1, source_target_pairs={{0,64},{8,72},{16,80},{24,88},{32,96},{40,104},{48,112},{56,120},{... | collective-permute-start | bytes 129032
  626.1 39.8 %collective-permute-start.4 = (f32[128,96]{0,1:T(8,128)S(1)}, f32[128,96]{0,1:T(8,128)S(1)}, u32[]{:S(2)}, u32[]{:S(2)}) collective-permute-start(f32[128,96]{0,1:T(8,128)S(1)} %fusion), channel_id=1, source_target_pairs={{0,40},{8,48},{16,56},{24,64},{32,72},{40,80},{48,88},{56,96},{64,... | collective-permute-start | bytes 147464
  641.5 24.4 %collective-permute-start.3 = (f32[128,96]{0,1:T(8,128)S(1)}, f32[128,96]{0,1:T(8,128)S(1)}, u32[]{:S(2)}, u32[]{:S(2)}) collective-permute-start(f32[128,96]{0,1:T(8,128)S(1)} %fusion), channel_id=1, source_target_pairs={{0,32},{8,40},{16,48},{24,56},{32,64},{40,72},{48,80},{56,88},{64,... | collective-permute-start | bytes 147464
  652.4 13.6 %collective-permute-start.2 = (f32[128,96]{0,1:T(8,128)S(1)}, f32[128,96]{0,1:T(8,128)S(1)}, u32[]{:S(2)}, u32[]{:S(2)}) collective-permute-start(f32[128,96]{0,1:T(8,128)S(1)} %fusion), channel_id=1, source_target_pairs={{0,24},{8,32},{16,40},{24,48},{32,56},{40,64},{48,72},{56,80},{64,... | collective-permute-start | bytes 147464
  654.3 13.7 %collective-permute-start.1 = (f32[128,96]{0,1:T(8,128)S(1)}, f32[128,96]{0,1:T(8,128)S(1)}, u32[]{:S(2)}, u32[]{:S(2)}) collective-permute-start(f32[128,96]{0,1:T(8,128)S(1)} %fusion), channel_id=1, source_target_pairs={{0,16},{8,24},{16,32},{24,40},{32,48},{40,56},{48,64},{56,72},{64,... | collective-permute-start | bytes 147464
  660.6 9.0 %collective-permute-start = (f32[128,96]{0,1:T(8,128)S(1)}, f32[128,96]{0,1:T(8,128)S(1)}, u32[]{:S(2)}, u32[]{:S(2)}) collective-permute-start(f32[128,96]{0,1:T(8,128)S(1)} %fusion), channel_id=1, source_target_pairs={{0,8},{8,16},{16,24},{24,32},{32,40},{40,48},{48,56},{56,64},{64,7... | collective-permute-start | bytes 147464
Sparse Core Ops, SparseCore 0:
  10.1 272.0 all-gather.8
  284.3 95.7 all-gather.4
  424.1 51.9 all-gather.6
where the time goes:
time: 681 us; the launch traced here: 682 us
  waiting for transfers between devices  363 us (53%)
  blocking collectives  186 us (27%)
  starting transfers between devices  69.3 us (10%)
  matrix products  19.7 us (3%)
  local copies, waits for them, and re-layouts  17.3 us (3%)
  between operations  17.2 us (3%)
  other arithmetic  9.23 us (1%)
    all_gather x1, waiting for transfers between devices, on_device(): table = lax.all_gather(embedding, ('dp', 'ctx'), axis=1, tiled=True)  269 us
    unnamed x1, blocking collectives  158 us
    all_gather x1, waiting for transfers between devices, on_device(): whole = lax.all_gather(hidden, 'vocab', axis=1, tiled=True)  88.8 us
    unnamed x8, starting transfers between devices  63.3 us
    pmax x1, blocking collectives, on_device(): peak = lax.pmax(local_max, 'vocab')  14.2 us
    psum x1, blocking collectives, on_device(): total, target_logit = lax.psum((local_sum, target_part), 'vocab')  14.2 us
  transfers between devices with their start and end apart: 12, of which 4 were waited for; matrix products, arithmetic and copies ran while one was open for 29% of the time, Pallas kernels for 0%

commit v1 on v0

v1 whole, which is shorter than its diff:
```python
import jax
import jax.numpy as jnp
from jax import lax
from jax.experimental import pallas as pl
from jax.experimental.pallas import tpu as pltpu
from jax.sharding import PartitionSpec as P

MESH = pl.DeviceIdType.MESH
BF = jnp.bfloat16
F32 = jnp.float32
DEAD = -1e30
NX, NL, NZ, NH, NC = 4, 2, 8, 4, 2
TILE = 128
HALF = 64
TOK = 512
FEAT = 672
PIECE = 84
PAD = 96
HROW = FEAT // 2
NSEM = 128


def nt(a, b):
    return lax.dot_general(a, b, (((1,), (1,)), ((), ())), preferred_element_type=F32)


def nn(a, b):
    return jnp.dot(a, b, preferred_element_type=F32)


def iotas(shape):
    return lax.broadcasted_iota(jnp.int32, shape, 0), lax.broadcasted_iota(jnp.int32, shape, 1)


def mask_bf16(cond):
    return jnp.where(cond, 1.0, 0.0).astype(BF)


def kernel(
    hid, emb, tgt, pat, lgr, loss_o, hg_o, eg_o,
    piece, stage, sel, selt, hidt, et, sbuf, sib, opp, opp_a, opp_b, nbr_p, nbr_m, in_p, in_m, lsum,
    gbuf, lbuf, xo, xs, xin, tbuf, pieces, pin, ssem, rsem,
):
    x = lax.axis_index("dp")
    ctx = lax.axis_index("ctx")
    v = lax.axis_index("vocab")
    l, z = lax.div(ctx, NZ), lax.rem(ctx, NZ)
    h, c = lax.div(v, NC), lax.rem(v, NC)

    def dev(x, l, z, h, c):
        return (x, l * NZ + z, h * NC + c)

    def add(a, d, n):
        return lax.rem(a + d, n)

    sibling = dev(x, l, z, h, 1 - c)
    hp, hm = dev(x, l, z, add(h, 1, NH), c), dev(x, l, z, add(h, 3, NH), c)
    xp, xm = dev(add(x, 1, NX), l, z, h, c), dev(add(x, 3, NX), l, z, h, c)
    yl = dev(x, 1 - l, z, h, c)
    diag = jnp.logical_and(x == h, l == c)
    off_diag = jnp.logical_not(diag)

    bar = pltpu.get_barrier_semaphore()

    def greet(who):
        pl.semaphore_signal(bar, inc=1, device_id=who, device_id_type=MESH)

    others = [(dq, dc) for dq in range(NH) for dc in range(NC) if dq or dc]
    others_dev = [dev(x, l, z, add(h, dq, NH), add(c, dc, NC)) for dq, dc in others]
    turned = [dev(h, c, add(z, d, NZ), x, l) for d in range(NZ)]
    away = [dev(h, c, add(z, d, NZ), x, 1 - l) for d in range(NZ)]
    away_src = [dev(h, 1 - c, add(z, d, NZ), x, l) for d in range(NZ)]
    for who in others_dev + [xp, xm, yl] + turned[1:] + away_src:
        greet(who)

    @pl.when(off_diag)
    def _():
        greet(turned[0])

    count = [0]
    sent = []

    def copy(src, dst, to):
        i = count[0]
        count[0] += 1
        return pltpu.make_async_remote_copy(
            src_ref=src, dst_ref=dst, send_sem=ssem.at[i], recv_sem=rsem.at[i],
            device_id=to, device_id_type=MESH,
        )

    def send(src, dst, to):
        cp = copy(src, dst, to)
        cp.start()
        sent.append(cp)
        return cp

    a, b = iotas((PAD, PIECE))
    piece[...] = nt(mask_bf16(a == b), emb[...]).astype(BF)

    peers = len(others) + 3 + (NZ - 1) + NZ
    pl.semaphore_wait(bar, jnp.where(off_diag, peers + 1, peers))

    first = [copy(piece, stage.at[z], turned[0])]

    @pl.when(off_diag)
    def _():
        first[0].start()

    for d in range(1, NZ):
        first.append(send(piece, stage.at[z], turned[d]))

    @pl.when(diag)
    def _():
        stage[z] = piece[...]

    a, b = iotas((FEAT, NZ * PAD))
    q = (b * 683) >> 16
    sel[...] = mask_bf16(jnp.logical_and(b - PAD * q < PIECE, a == b - (PAD - PIECE) * q))
    b, a = iotas((NZ * PAD, FEAT))
    q = (b * 683) >> 16
    selt[...] = mask_bf16(jnp.logical_and(b - PAD * q < PIECE, a == b - (PAD - PIECE) * q))
    a, b = iotas((FEAT, FEAT))
    hidt[...] = nt(mask_bf16(a == b), hid[...]).astype(BF)

    @pl.when(off_diag)
    def _():
        first[0].wait()

    for cp in first[1:]:
        cp.wait_recv()
    et[0] = nn(sel[...], stage[...].reshape(NZ * PAD, TILE)).astype(BF)

    rows2 = [pl.ds(0, HROW), pl.ds(HROW, HROW)]

    def pass_on(src, dst, to, half):
        return send(et.at[src, rows2[half]], et.at[dst, rows2[half]], to)

    a1, a2, a3, b2, b3, c2, c3 = [], [], [], [], [], [], []
    for half in range(2):
        a1.append(pass_on(0, 1, yl, half))
        a2.append(pass_on(0, 6, xp, half))
        a3.append(pass_on(0, 2, xm, half))
    for half in range(2):
        a1[half].wait_recv()
        b2.append(pass_on(1, 7, xp, half))
        b3.append(pass_on(1, 3, xm, half))
        a3[half].wait_recv()
        c3.append(pass_on(2, 4, xm, half))

    sib_cp, opp_cp, nbr_cp = {}, {}, {}

    def weights(r):
        return jnp.concatenate([et[2 * r], et[2 * r + 1]], axis=1)

    def logits(r):
        s = nn(hid[...], weights(r))
        base = lax.rem(x + r, NX) * 2
        _, lane = iotas((TILE, 2 * TILE))
        block = base + jnp.where(lane < TILE, l, 1 - l)
        for t in range(NH):
            off = jnp.logical_and(block == v, pat[t : t + 1, 0:1] == 0)
            part = jnp.where(off, DEAD, s[t * TILE : (t + 1) * TILE])
            sbuf[r, t] = part.reshape(NC, HALF, 2 * TILE)
        sib_cp[r] = send(sbuf.at[r, :, 1 - c], sib.at[r], sibling)

    def mine(r, dq, rows=slice(None)):
        t = add(h, dq, NH)
        return sbuf[r, t, c, rows] + sib[r, t, rows]

    lo, hi = pl.ds(0, HALF // 2), pl.ds(HALF // 2, HALF // 2)

    def to_far(r):
        sib_cp[r].wait_recv()
        opp[r] = mine(r, 2)
        opp_cp[r] = (
            send(opp.at[r, lo], opp_a.at[r], hp),
            send(opp.at[r, hi], opp_b.at[r], hm),
        )

    def to_near(r):
        near_p, near_m = mine(r, 1), mine(r, 3)
        opp_cp[r][0].wait_recv()
        nbr_p[r] = jnp.concatenate([near_p[: HALF // 2] + opp_a[r], near_p[HALF // 2 :]], axis=0)
        p = send(nbr_p.at[r], in_p.at[r], hp)
        opp_cp[r][1].wait_recv()
        nbr_m[r] = jnp.concatenate([near_m[: HALF // 2], near_m[HALF // 2 :] + opp_b[r]], axis=0)
        nbr_cp[r] = (p, send(nbr_m.at[r], in_m.at[r], hm))

    def whole(r):
        own = mine(r, 0)
        nbr_cp[r][0].wait_recv()
        nbr_cp[r][1].wait_recv()
        lsum[r] = own + in_p[r] + in_m[r]

    logits(0)
    b2[0].wait_recv()
    c2.append(pass_on(7, 5, xp, 0))
    to_far(0)
    b2[1].wait_recv()
    c2.append(pass_on(7, 5, xp, 1))
    for cp in b3:
        cp.wait_recv()
    logits(1)
    for cp in a2:
        cp.wait_recv()
    logits(3)
    to_near(0)
    to_far(1)
    to_far(3)
    to_near(1)
    to_near(3)
    for cp in c3 + c2:
        cp.wait_recv()
    logits(2)
    to_far(2)
    whole(0)
    whole(1)
    whole(3)
    to_near(2)
    whole(2)

    sub, lane = iotas((HALF, TILE))
    turn = sub + c * HALF == lane

    def column(row):
        return jnp.sum(jnp.where(turn, row, 0.0), axis=1, keepdims=True)

    target = column(tgt[pl.ds(h, 1), :].astype(F32)).astype(jnp.int32)
    scale = column(lgr[pl.ds(h, 1), :])
    _, lane2 = iotas((HALF, 2 * TILE))
    hits, ls = [], []
    for r in range(NX):
        col = lax.rem(x + r, NX) * 2 * TILE + jnp.where(lane2 < TILE, l, 1 - l) * TILE
        hits.append(col + jnp.where(lane2 < TILE, lane2, lane2 - TILE) == target)
        ls.append(lsum[r])
    peak = jnp.max(jnp.maximum(jnp.maximum(ls[0], ls[1]), jnp.maximum(ls[2], ls[3])), axis=1, keepdims=True)
    total = sum(jnp.exp(s - peak) for s in ls)
    total = jnp.sum(total, axis=1, keepdims=True)
    lse = peak + jnp.log(total)
    at_target = sum(jnp.where(hit, s, 0.0) for hit, s in zip(hits, ls))
    loss = lse - jnp.sum(at_target, axis=1, keepdims=True)
    own_rows = pl.ds(pl.multiple_of(h * TILE + c * HALF, HALF), HALF)
    order = (2, 1, 3, 0)
    g_sib, g_p, g_m, f_p, f_m, relay = {}, {}, {}, {}, {}, {}
    for r in order:
        probs = jnp.exp(ls[r] - lse)
        gbuf[r, own_rows] = (scale * (probs - jnp.where(hits[r], 1.0, 0.0))).astype(BF)
        mine_g = gbuf.at[r, own_rows]
        g_p[r] = send(mine_g, mine_g, hp)
        g_m[r] = send(mine_g, mine_g, hm)
        g_sib[r] = send(mine_g, mine_g, sibling)
    loss_row = jnp.sum(jnp.where(turn, loss, 0.0), axis=0, keepdims=True)
    lbuf[v] = jnp.broadcast_to(loss_row, (8, TILE))
    loss_cp = [send(lbuf.at[v], lbuf.at[v], who) for who in others_dev]

    def rows_of(dq, start, size):
        return pl.ds(pl.multiple_of(add(h, dq, NH) * TILE + c * HALF + start, size), size)

    def forward(r):
        g_p[r].wait_recv()
        near_m = gbuf.at[r, rows_of(3, HALF // 2, HALF // 2)]
        f_p[r] = send(near_m, near_m, hp)
        g_m[r].wait_recv()
        near_p = gbuf.at[r, rows_of(1, 0, HALF // 2)]
        f_m[r] = send(near_p, near_p, hm)
        relay[r] = []
        for dq in (3, 1):
            part = gbuf.at[r, rows_of(dq, 0, HALF)]
            relay[r].append(send(part, part, sibling))

    def forward_far(r):
        f_p[r].wait_recv()
        f_m[r].wait_recv()
        part = gbuf.at[r, rows_of(2, 0, HALF)]
        relay[r].append(send(part, part, sibling))

    def gathered(r):
        g_sib[r].wait_recv()
        for cp in relay[r]:
            cp.wait_recv()

    def grad(r):
        return nn(hidt[...], gbuf[r])

    x_cp = {}
    forward(2)
    forward(1)
    forward_far(2)
    gathered(2)
    d = grad(2)
    xo[0] = d[:, :TILE].astype(BF)
    x_cp["far_p"] = send(xo.at[0], xin.at[0], xp)
    xo[1] = d[:, TILE:].astype(BF)
    x_cp["far_m"] = send(xo.at[1], xin.at[1], xm)
    forward(3)
    forward_far(1)
    gathered(1)
    d = grad(1)
    xo[2] = d[:, TILE:].astype(BF)
    x_cp["p1"] = send(xo.at[2], xin.at[2], xp)
    tbuf[0] = d[:, :TILE]
    forward(0)
    forward_far(3)
    gathered(3)
    d = grad(3)
    xo[3] = d[:, :TILE].astype(BF)
    x_cp["m0"] = send(xo.at[3], xin.at[3], xm)
    tbuf[1] = d[:, TILE:]
    x_cp["far_p"].wait_recv()
    xs[0] = (tbuf[0] + xin[0].astype(F32)).astype(BF)
    x_cp["p0"] = send(xs.at[0], xin.at[4], xp)
    x_cp["far_m"].wait_recv()
    xs[1] = (tbuf[1] + xin[1].astype(F32)).astype(BF)
    x_cp["m1"] = send(xs.at[1], xin.at[5], xm)
    forward_far(0)
    gathered(0)
    d = grad(0)
    tbuf[0] = d[:, :TILE]
    tbuf[1] = d[:, TILE:]

    hg = nt(gbuf[0], weights(0))
    for r in range(1, NX):
        hg = hg + nt(gbuf[r], weights(r))
    hg_o[...] = hg.astype(BF)
    for cp in loss_cp:
        cp.wait_recv()
    for t in range(NH):
        loss_o[t : t + 1, :] = lbuf[2 * t, 0:1, :] + lbuf[2 * t + 1, 0:1, :]

    last = [[], []]
    for m, (near, far) in enumerate(((4, 3), (2, 5))):
        x_cp[("p0", "p1")[m]].wait_recv()
        x_cp[("m0", "m1")[m]].wait_recv()
        tot = tbuf[m] + xin[near].astype(F32) + xin[far].astype(F32)
        pieces[m] = nn(selt[...], tot.astype(BF)).astype(BF).reshape(NZ, PAD, TILE)
        for d in range(NZ):
            cp = copy(pieces.at[m, add(z, d, NZ)], pin.at[m, z], (turned, away)[m][d])
            last[m].append(cp)
            if d or m:
                cp.start()
                sent.append(cp)

    @pl.when(off_diag)
    def _():
        last[0][0].start()

    @pl.when(diag)
    def _():
        pin[0, z] = pieces[0, z]

    for cp in last[0][1:] + last[1]:
        cp.wait_recv()

    @pl.when(off_diag)
    def _():
        last[0][0].wait()

    acc = None
    for m in range(2):
        for zz in range(NZ):
            p = pin[m, zz].astype(F32)
            acc = p if acc is None else acc + p
    full = jnp.concatenate([acc, jnp.zeros((TILE - PAD, TILE), F32)], axis=0)
    eg_o[...] = full.T[:, :PIECE]
    for cp in sent:
        cp.wait_send()


def on_device(hidden, embedding, targets, pattern, loss_grad):
    vmem = pl.BlockSpec(memory_space=pltpu.VMEM)
    loss, hidden_grad, embedding_grad = pl.pallas_call(
        kernel,
        out_shape=(
            jax.ShapeDtypeStruct((NH, TILE), F32),
            jax.ShapeDtypeStruct((TOK, FEAT), BF),
            jax.ShapeDtypeStruct((TILE, PIECE), F32),
        ),
        in_specs=[vmem] * 5,
        out_specs=(vmem,) * 3,
        scratch_shapes=[
            pltpu.VMEM((PAD, TILE), BF),
            pltpu.VMEM((NZ, PAD, TILE), BF),
            pltpu.VMEM((FEAT, NZ * PAD), BF),
            pltpu.VMEM((NZ * PAD, FEAT), BF),
            pltpu.VMEM((FEAT, TOK), BF),
            pltpu.VMEM((8, FEAT, TILE), BF),
            pltpu.VMEM((NX, NH, NC, HALF, 2 * TILE), F32),
            pltpu.VMEM((NX, NH, HALF, 2 * TILE), F32),
            pltpu.VMEM((NX, HALF, 2 * TILE), F32),
            pltpu.VMEM((NX, HALF // 2, 2 * TILE), F32),
            pltpu.VMEM((NX, HALF // 2, 2 * TILE), F32),
            pltpu.VMEM((NX, HALF, 2 * TILE), F32),
            pltpu.VMEM((NX, HALF, 2 * TILE), F32),
            pltpu.VMEM((NX, HALF, 2 * TILE), F32),
            pltpu.VMEM((NX, HALF, 2 * TILE), F32),
            pltpu.VMEM((NX, HALF, 2 * TILE), F32),
            pltpu.VMEM((NX, TOK, 2 * TILE), BF),
            pltpu.VMEM((NH * NC, 8, TILE), F32),
            pltpu.VMEM((4, FEAT, TILE), BF),
            pltpu.VMEM((2, FEAT, TILE), BF),
            pltpu.VMEM((6, FEAT, TILE), BF),
            pltpu.VMEM((2, FEAT, TILE), F32),
            pltpu.VMEM((2, NZ, PAD, TILE), BF),
            pltpu.VMEM((2, NZ, PAD, TILE), BF),
            pltpu.SemaphoreType.DMA((NSEM,)),
            pltpu.SemaphoreType.DMA((NSEM,)),
        ],
        compiler_params=pltpu.CompilerParams(
            collective_id=0, has_side_effects=True, vmem_limit_bytes=48 << 20
        ),
    )(hidden, embedding, targets.reshape(NH, TILE), pattern, loss_grad.reshape(NH, TILE))
    return loss.reshape(TOK), hidden_grad, embedding_grad


def solution(mesh):
    return jax.shard_map(
        on_device,
        mesh=mesh,
        in_specs=(
            P(("dp", "ctx"), "vocab"),
            P("vocab", ("dp", "ctx")),
            P(("dp", "ctx")),
            P(("dp", "ctx"), "vocab"),
            P(("dp", "ctx")),
        ),
        out_specs=(P(("dp", "ctx")), P(("dp", "ctx"), "vocab"), P("vocab", ("dp", "ctx"))),
        check_vma=False,
    )
```

time: 681 us -> 153 us (0.22)
  the two profiles are of different devices: /device:TPU:4 before, /device:TPU:8 now
where the time goes in v1:
time: 153 us
  Pallas kernels  147 us (96%)
  local copies, waits for them, and re-layouts  5.38 us (4%)
    pallas_call x1, Pallas kernels, on_device(): pl.pallas_call(kernel, out_shape=(jax.ShapeDtypeStruct((NH, TILE), F32),...  147 us
    unnamed x12, local copies, waits for them, and re-layouts  5.38 us

profile of v1, /device:TPU:8, one launch (start us, length us, event | category | flops | bytes accessed | tf_op | source)
XLA Modules:
  0.0 152.8 jit_solution(11923511765622788812)
XLA Ops:
  0.6 0.0 copy-start.2
  0.6 0.6 copy-done.2
  1.3 0.1 copy.10.pat
  1.4 0.8 copy.9.emb
  2.2 0.0 copy-start
  2.2 0.0 copy-start.1
  2.2 1.4 copy.8.hid
  3.6 0.0 copy-done
  3.6 0.0 copy-done.1
  3.7 146.8 %shard_map.76 = (f32[4,128]{1,0:T(4,128)S(1)}, bf16[512,672]{1,0:T(8,128)(2,1)S(1)}, f32[128,84]{1,0:T(8,128)S(1)}) custom-call(bf16[512,672]{1,0:T(8,128)(2,1)S(1)} %copy.8.hid, bf16[128,84]{1,0:T(8,128)(2,1)S(1)} %copy.9.emb, s32[4,128]{1,0:T(4,128)S(1)} %bitcast.3, s32[4,1]{1,0:T(4,128)S(1)} %copy.10.pat, f32[4,128]{1,0:T(4,128)S(1)} %bitcast.4), custom_call_target="tpu_custom_call" | custom-call | tf_op jit(solution)/shard_map/pallas_call | solution.py:371
  150.4 0.7 copy.12
  151.1 1.1 copy.11
  152.2 0.6 copy.14
Async XLA Ops:
  0.6 0.7 copy-start.2
  2.2 1.4 copy-start
  2.2 1.4 copy-start.1

commit v2 on v1

v2 whole, which is shorter than its diff:
```python
import jax
import jax.numpy as jnp
from jax import lax
from jax.experimental import pallas as pl
from jax.experimental.pallas import tpu as pltpu
from jax.sharding import PartitionSpec as P

MESH = pl.DeviceIdType.MESH
BF = jnp.bfloat16
F32 = jnp.float32
I16 = jnp.int16
DEAD = -1e30
TOP = 32767.0
NX, NL, NZ, NH, NC = 4, 2, 8, 4, 2
TILE = 128
HALF = 64
WIDE = 2 * TILE
TOK = 512
FEAT = 672
PIECE = 84
PAD = 96
HROW = FEAT // 2
NSEM = 128


def nt(a, b):
    return lax.dot_general(a, b, (((1,), (1,)), ((), ())), preferred_element_type=F32)


def nn(a, b):
    return jnp.dot(a, b, preferred_element_type=F32)


def iotas(shape):
    return lax.broadcasted_iota(jnp.int32, shape, 0), lax.broadcasted_iota(jnp.int32, shape, 1)


def mask_bf16(cond):
    return jnp.where(cond, 1.0, 0.0).astype(BF)


def largest(a):
    return jnp.max(jnp.max(a, axis=1, keepdims=True), axis=0, keepdims=True)


def kernel(
    hidt, embt, tgt, pat, lgr, loss_o, hg_o, eg_o,
    piece, stage, sel, selt, hid, et, sbuf, sib, qout, qstep, qin, qin_step, lsum,
    gbuf, lbuf, xo, xs, xin, tbuf, pieces, pin, zsum, fin, ssem, rsem,
):
    x = lax.axis_index("dp")
    ctx = lax.axis_index("ctx")
    v = lax.axis_index("vocab")
    l, z = lax.div(ctx, NZ), lax.rem(ctx, NZ)
    h, c = lax.div(v, NC), lax.rem(v, NC)

    def dev(x, l, z, h, c):
        return (x, l * NZ + z, h * NC + c)

    def add(a, d, n):
        return lax.rem(a + d, n)

    sibling = dev(x, l, z, h, 1 - c)
    ring_h = [dev(x, l, z, add(h, dq, NH), c) for dq in range(NH)]
    xp, xm = dev(add(x, 1, NX), l, z, h, c), dev(add(x, 3, NX), l, z, h, c)
    yl = dev(x, 1 - l, z, h, c)
    ring_z = [dev(x, l, add(z, d, NZ), h, c) for d in range(NZ)]
    turned = dev(h, c, z, x, l)
    away, away_src = dev(h, c, z, x, 1 - l), dev(h, 1 - c, z, x, l)
    diag = jnp.logical_and(x == h, l == c)
    off_diag = jnp.logical_not(diag)

    bar = pltpu.get_barrier_semaphore()

    def greet(who):
        pl.semaphore_signal(bar, inc=1, device_id=who, device_id_type=MESH)

    others = [(dq, dc) for dq in range(NH) for dc in range(NC) if dq or dc]
    others_dev = [dev(x, l, z, add(h, dq, NH), add(c, dc, NC)) for dq, dc in others]
    met = others_dev + [xp, xm, yl] + ring_z[1:] + [away_src]

    @pl.when(off_diag)
    def _():
        greet(turned)

    for who in met:
        greet(who)

    count = [0]
    sent = []

    def copy(src, dst, to):
        i = count[0]
        count[0] += 1
        cp = pltpu.make_async_remote_copy(
            src_ref=src, dst_ref=dst, send_sem=ssem.at[i], recv_sem=rsem.at[i],
            device_id=to, device_id_type=MESH,
        )
        return cp

    def send(src, dst, to):
        cp = copy(src, dst, to)
        cp.start()
        sent.append(cp)
        return cp

    piece[...] = jnp.zeros((PAD, TILE), BF)
    piece[:PIECE] = embt[...]
    pl.semaphore_wait(bar, jnp.where(off_diag, len(met) + 1, len(met)))
    swap = copy(piece, stage.at[z], turned)

    @pl.when(off_diag)
    def _():
        swap.start()

    @pl.when(diag)
    def _():
        stage[z] = piece[...]

    a, b = iotas((FEAT, NZ * PAD))
    q = (b * 683) >> 16
    sel[...] = mask_bf16(jnp.logical_and(b - PAD * q < PIECE, a == b - (PAD - PIECE) * q))

    @pl.when(off_diag)
    def _():
        swap.wait()

    over_z = [send(stage.at[z], stage.at[z], ring_z[d]) for d in (4, 3, 5, 2, 6, 1, 7)]
    a, b = iotas((TOK, TOK))
    hid[...] = nt(mask_bf16(a == b), hidt[...]).astype(BF)
    b, a = iotas((NZ * PAD, FEAT))
    q = (b * 683) >> 16
    selt[...] = mask_bf16(jnp.logical_and(b - PAD * q < PIECE, a == b - (PAD - PIECE) * q))
    for cp in over_z:
        cp.wait_recv()
    et[0] = nn(sel[...], stage[...].reshape(NZ * PAD, TILE)).astype(BF)

    rows2 = [pl.ds(0, HROW), pl.ds(HROW, HROW)]

    def pass_on(src, dst, to, half):
        return send(et.at[src, rows2[half]], et.at[dst, rows2[half]], to)

    a1, a2, a3, b2, b3, c2, c3 = [], [], [], [], [], [], []
    for half in range(2):
        a1.append(pass_on(0, 1, yl, half))
        a2.append(pass_on(0, 6, xp, half))
        a3.append(pass_on(0, 2, xm, half))
    for half in range(2):
        a1[half].wait_recv()
        b2.append(pass_on(1, 7, xp, half))
        b3.append(pass_on(1, 3, xm, half))
        a3[half].wait_recv()
        c3.append(pass_on(2, 4, xm, half))

    def weights(r):
        return jnp.concatenate([et[2 * r], et[2 * r + 1]], axis=1)

    sib_cp, q_cp = {}, {}

    def logits(r):
        s = nn(hid[...], weights(r))
        base = lax.rem(x + r, NX) * 2
        _, lane = iotas((TILE, WIDE))
        block = base + jnp.where(lane < TILE, l, 1 - l)
        for t in range(NH):
            off = jnp.logical_and(block == v, pat[0:1, t : t + 1] == 0)
            part = jnp.where(off, DEAD, s[t * TILE : (t + 1) * TILE])
            sbuf[r, t] = part.reshape(NC, HALF, WIDE)
        sib_cp[r] = send(sbuf.at[r, :, 1 - c], sib.at[r], sibling)

    def mine(r, dq):
        t = add(h, dq, NH)
        return sbuf[r, t, c] + sib[r, t]

    def spread(r):
        sib_cp[r].wait_recv()
        q_cp[r] = []
        for dq in (2, 1, 3):
            s = mine(r, dq)
            dead = s < 0.5 * DEAD
            peak = largest(jnp.where(dead, 0.0, jnp.abs(s)))
            step = jnp.maximum(peak, 1e-30) * (1.0 / TOP)
            steps = jnp.clip(jnp.round(s * (1.0 / step)), -TOP, TOP)
            qout[r, dq - 1] = jnp.where(dead, -TOP - 1.0, steps).astype(jnp.int32).astype(I16)
            qstep[r, dq - 1] = jnp.broadcast_to(step, (8, TILE))
            q_cp[r].append(send(qstep.at[r, dq - 1], qin_step.at[r, dq - 1], ring_h[dq]))
            q_cp[r].append(send(qout.at[r, dq - 1], qin.at[r, dq - 1], ring_h[dq]))

    def whole(r):
        total = mine(r, 0)
        for cp in q_cp[r]:
            cp.wait_recv()
        for k in range(NH - 1):
            steps = qin[r, k].astype(jnp.int32).astype(F32)
            total = total + jnp.where(steps < -TOP - 0.5, DEAD, steps * qin_step[r, k, 0:1, 0:1])
        lsum[r] = total

    logits(0)
    b2[0].wait_recv()
    c2.append(pass_on(7, 5, xp, 0))
    spread(0)
    b2[1].wait_recv()
    c2.append(pass_on(7, 5, xp, 1))
    for cp in b3:
        cp.wait_recv()
    logits(1)
    for cp in a2:
        cp.wait_recv()
    logits(3)
    spread(1)
    spread(3)
    for cp in c3 + c2:
        cp.wait_recv()
    logits(2)
    whole(0)
    spread(2)
    whole(1)
    whole(3)
    whole(2)

    sub, lane = iotas((HALF, TILE))
    turn = sub + c * HALF == lane

    def column(row):
        return jnp.sum(jnp.where(turn, row, 0.0), axis=1, keepdims=True)

    target = column(tgt[pl.ds(h, 1), :].astype(F32)).astype(jnp.int32)
    scale = column(lgr[pl.ds(h, 1), :])
    _, lane2 = iotas((HALF, WIDE))
    hits, ls = [], []
    for r in range(NX):
        col = lax.rem(x + r, NX) * WIDE + jnp.where(lane2 < TILE, l, 1 - l) * TILE
        hits.append(col + jnp.where(lane2 < TILE, lane2, lane2 - TILE) == target)
        ls.append(lsum[r])
    peak = jnp.maximum(jnp.maximum(ls[0], ls[1]), jnp.maximum(ls[2], ls[3]))
    peak = jnp.max(peak, axis=1, keepdims=True)
    total = jnp.sum(sum(jnp.exp(s - peak) for s in ls), axis=1, keepdims=True)
    lse = peak + jnp.log(total)
    at_target = sum(jnp.where(hit, s, 0.0) for hit, s in zip(hits, ls))
    loss = lse - jnp.sum(at_target, axis=1, keepdims=True)
    g_cp, relay = {}, {}
    for r in (2, 1, 3, 0):
        probs = jnp.exp(ls[r] - lse)
        gbuf[r, h, c] = (scale * (probs - jnp.where(hits[r], 1.0, 0.0))).astype(BF)
        own = gbuf.at[r, h, c]
        g_cp[r] = [send(own, own, ring_h[dq]) for dq in (2, 1, 3)]
    loss_row = jnp.sum(jnp.where(turn, loss, 0.0), axis=0, keepdims=True)
    lbuf[v] = jnp.broadcast_to(loss_row, (8, TILE))
    loss_cp = [send(lbuf.at[v], lbuf.at[v], who) for who in others_dev]

    def pair(r):
        for cp in g_cp[r]:
            cp.wait_recv()
        part = gbuf.at[r, :, c]
        relay[r] = send(part, part, sibling)

    def grad(r):
        relay[r].wait_recv()
        return nn(hidt[...], gbuf[r].reshape(TOK, WIDE))

    pair(2)
    d = grad(2)
    xo[0] = d[:, :TILE].astype(BF)
    far_p = send(xo.at[0], xin.at[0], xp)
    xo[1] = d[:, TILE:].astype(BF)
    far_m = send(xo.at[1], xin.at[1], xm)
    pair(1)
    d = grad(1)
    xo[2] = d[:, TILE:].astype(BF)
    p1 = send(xo.at[2], xin.at[2], xp)
    tbuf[0] = d[:, :TILE]
    pair(3)
    d = grad(3)
    xo[3] = d[:, :TILE].astype(BF)
    m0 = send(xo.at[3], xin.at[3], xm)
    tbuf[1] = d[:, TILE:]
    pair(0)
    far_p.wait_recv()
    xs[0] = (tbuf[0] + xin[0].astype(F32)).astype(BF)
    p0 = send(xs.at[0], xin.at[4], xp)
    far_m.wait_recv()
    xs[1] = (tbuf[1] + xin[1].astype(F32)).astype(BF)
    m1 = send(xs.at[1], xin.at[5], xm)
    d = grad(0)
    tbuf[0] = d[:, :TILE]
    tbuf[1] = d[:, TILE:]

    hg = nt(weights(0), gbuf[0].reshape(TOK, WIDE))
    for r in range(1, NX):
        hg = hg + nt(weights(r), gbuf[r].reshape(TOK, WIDE))
    hg_o[...] = hg.astype(BF)
    for cp in loss_cp:
        cp.wait_recv()
    for t in range(NH):
        loss_o[t : t + 1, :] = lbuf[2 * t, 0:1, :] + lbuf[2 * t + 1, 0:1, :]

    z_cp = [[], []]
    for m, (near, far) in ((1, (p1, m1)), (0, (m0, p0))):
        near.wait_recv()
        far.wait_recv()
        tot = tbuf[m] + xin[(3, 2)[m]].astype(F32) + xin[(4, 5)[m]].astype(F32)
        pieces[m] = nn(selt[...], tot.astype(BF)).astype(BF).reshape(NZ, PAD, TILE)
        for d in (4, 3, 5, 2, 6, 1, 7):
            z_cp[m].append(send(pieces.at[m, add(z, d, NZ)], pin.at[m, z], ring_z[d]))
        pin[m, z] = pieces[m, z]

    def over_z_sum(m):
        for cp in z_cp[m]:
            cp.wait_recv()
        total = pin[m, 0].astype(F32)
        for k in range(1, NZ):
            total = total + pin[m, k].astype(F32)
        zsum[m] = total.astype(BF)

    over_z_sum(1)
    end1 = send(zsum.at[1], fin.at[1], away)
    over_z_sum(0)
    end0 = copy(zsum.at[0], fin.at[0], turned)

    @pl.when(off_diag)
    def _():
        end0.start()

    @pl.when(diag)
    def _():
        fin[0] = zsum[0]

    end1.wait_recv()

    @pl.when(off_diag)
    def _():
        end0.wait()

    eg_o[...] = (fin[0].astype(F32) + fin[1].astype(F32))[:PIECE]
    for cp in sent:
        cp.wait_send()


def on_device(hidden, embedding, targets, pattern, loss_grad):
    vmem = pl.BlockSpec(memory_space=pltpu.VMEM)
    loss, hidden_grad, embedding_grad = pl.pallas_call(
        kernel,
        out_shape=(
            jax.ShapeDtypeStruct((NH, TILE), F32),
            jax.ShapeDtypeStruct((FEAT, TOK), BF),
            jax.ShapeDtypeStruct((PIECE, TILE), F32),
        ),
        in_specs=[vmem] * 5,
        out_specs=(vmem,) * 3,
        scratch_shapes=[
            pltpu.VMEM((PAD, TILE), BF),
            pltpu.VMEM((NZ, PAD, TILE), BF),
            pltpu.VMEM((FEAT, NZ * PAD), BF),
            pltpu.VMEM((NZ * PAD, FEAT), BF),
            pltpu.VMEM((TOK, FEAT), BF),
            pltpu.VMEM((8, FEAT, TILE), BF),
            pltpu.VMEM((NX, NH, NC, HALF, WIDE), F32),
            pltpu.VMEM((NX, NH, HALF, WIDE), F32),
            pltpu.VMEM((NX, NH - 1, HALF, WIDE), I16),
            pltpu.VMEM((NX, NH - 1, 8, TILE), F32),
            pltpu.VMEM((NX, NH - 1, HALF, WIDE), I16),
            pltpu.VMEM((NX, NH - 1, 8, TILE), F32),
            pltpu.VMEM((NX, HALF, WIDE), F32),
            pltpu.VMEM((NX, NH, NC, HALF, WIDE), BF),
            pltpu.VMEM((NH * NC, 8, TILE), F32),
            pltpu.VMEM((4, FEAT, TILE), BF),
            pltpu.VMEM((2, FEAT, TILE), BF),
            pltpu.VMEM((6, FEAT, TILE), BF),
            pltpu.VMEM((2, FEAT, TILE), F32),
            pltpu.VMEM((2, NZ, PAD, TILE), BF),
            pltpu.VMEM((2, NZ, PAD, TILE), BF),
            pltpu.VMEM((2, PAD, TILE), BF),
            pltpu.VMEM((2, PAD, TILE), BF),
            pltpu.SemaphoreType.DMA((NSEM,)),
            pltpu.SemaphoreType.DMA((NSEM,)),
        ],
        compiler_params=pltpu.CompilerParams(
            collective_id=0, has_side_effects=True, vmem_limit_bytes=48 << 20
        ),
    )(hidden.T, embedding.T, targets.reshape(NH, TILE), pattern.T, loss_grad.reshape(NH, TILE))
    return loss.reshape(TOK), hidden_grad.T, embedding_grad.T


def solution(mesh):
    return jax.shard_map(
        on_device,
        mesh=mesh,
        in_specs=(
            P(("dp", "ctx"), "vocab"),
            P("vocab", ("dp", "ctx")),
            P(("dp", "ctx")),
            P(("dp", "ctx"), "vocab"),
            P(("dp", "ctx")),
        ),
        out_specs=(P(("dp", "ctx")), P(("dp", "ctx"), "vocab"), P("vocab", ("dp", "ctx"))),
        check_vma=False,
    )
```

time: 153 us -> 100 us (0.65)
  the two profiles are of different devices: /device:TPU:8 before, /device:TPU:7 now
where the time goes in v2:
time: 100 us; the launch traced here: 98.2 us
  Pallas kernels  93 us (93%)
  local copies, waits for them, and re-layouts  4.55 us (5%)
    pallas_call x1, Pallas kernels, on_device(): pl.pallas_call(kernel, out_shape=(jax.ShapeDtypeStruct((NH, TILE), F32),...  93 us
    unnamed x13, local copies, waits for them, and re-layouts  4.55 us

profile of v2, /device:TPU:7, one launch (start us, length us, event | category | flops | bytes accessed | tf_op | source)
XLA Modules:
  0.0 98.2 jit_solution(9516797671872956742)
XLA Ops:
  0.6 0.0 copy-start.3
  0.6 0.0 copy-start.2
  0.7 0.0 copy-start.4
  0.7 0.7 copy-done.3
  1.3 0.0 copy-done.2
  1.3 0.0 copy-done.4
  1.3 0.0 copy-start
  1.3 1.1 %copy-done = bf16[512,672]{0,1:T(8,128)(2,1)S(1)} copy-done((bf16[512,672]{0,1:T(8,128)(2,1)S(1)}, bf16[512,672]{0,1:T(8,128)(2,1)}, u32[]{:S(2)}) %copy-start) | copy-done | bytes 688152
  2.4 0.0 copy-start.1
  2.4 0.7 copy-done.1
  3.2 93.0 %shard_map.76 = (f32[4,128]{1,0:T(4,128)S(1)}, bf16[672,512]{1,0:T(8,128)(2,1)S(1)}, f32[84,128]{1,0:T(8,128)S(1)}) custom-call(bf16[672,512]{1,0:T(8,128)(2,1)S(1)} %bitcast.8, bf16[84,128]{1,0:T(8,128)(2,1)S(1)} %bitcast.11, s32[4,128]{1,0:T(4,128)S(1)} %bitcast.12, s32[1,4]{1,0:T(1,128)S(1)} %bitcast.15, f32[4,128]{1,0:T(4,128)S(1)} %bitcast.13), custom_call_target="tpu_custom_call" | custom-call | tf_op jit(solution)/shard_map/pallas_call | solution.py:341
  96.2 0.6 copy.11
  96.8 0.8 copy.12
  97.6 0.6 copy.13
Async XLA Ops:
  0.6 0.7 copy-start.3
  0.6 0.7 copy-start.2
  0.7 0.7 copy-start.4
  1.3 1.1 %copy-start = (bf16[512,672]{0,1:T(8,128)(2,1)S(1)}, bf16[512,672]{0,1:T(8,128)(2,1)}, u32[]{:S(2)}) copy-start(bf16[512,672]{0,1:T(8,128)(2,1)} %param.5) | copy-start | bytes 2064388
  2.4 0.7 copy-start.1

commit v3 on v2

--- a/solution.py
+++ b/solution.py
@@ -19,14 +19,18 @@
 FEAT = 672
 PIECE = 84
 PAD = 96
-HROW = FEAT // 2
-NSEM = 128
+NSEM = 192
+ORDER_Z = (1, 7, 2, 6, 3, 5, 4)
 
 
 def nt(a, b):
     return lax.dot_general(a, b, (((1,), (1,)), ((), ())), preferred_element_type=F32)
 
 
+def tn(a, b):
+    return lax.dot_general(a, b, (((0,), (0,)), ((), ())), preferred_element_type=F32)
+
+
 def nn(a, b):
     return jnp.dot(a, b, preferred_element_type=F32)
 
@@ -35,18 +39,14 @@
     return lax.broadcasted_iota(jnp.int32, shape, 0), lax.broadcasted_iota(jnp.int32, shape, 1)
 
 
-def mask_bf16(cond):
-    return jnp.where(cond, 1.0, 0.0).astype(BF)
-
-
 def largest(a):
     return jnp.max(jnp.max(a, axis=1, keepdims=True), axis=0, keepdims=True)
 
 
 def kernel(
-    hidt, embt, tgt, pat, lgr, loss_o, hg_o, eg_o,
-    piece, stage, sel, selt, hid, et, sbuf, sib, qout, qstep, qin, qin_step, lsum,
-    gbuf, lbuf, xo, xs, xin, tbuf, pieces, pin, zsum, fin, ssem, rsem,
+    hidt_in, embt_in, tgt_in, pat_in, lgr_in, loss_o, hg_o, eg_o,
+    hidt, embt, tgt, pat, lgr, hidp, piece, et, sbuf, sib, qout, qstep, qin, qin_step, lsum,
+    gbuf, lbuf, xo, xin, pieces, pin, zsum, fin, ssem, rsem, lsem,
 ):
     x = lax.axis_index("dp")
     ctx = lax.axis_index("ctx")
@@ -67,6 +67,10 @@
     ring_z = [dev(x, l, add(z, d, NZ), h, c) for d in range(NZ)]
     turned = dev(h, c, z, x, l)
     away, away_src = dev(h, c, z, x, 1 - l), dev(h, 1 - c, z, x, l)
+    x2, h2 = add(x, 2, NX), add(h, 2, NX)
+    far = [dev(x2, l, z, h, c), dev(x2, 1 - l, z, h, c)]
+    far_away = [dev(h, c, z, x2, l), dev(h, c, z, x2, 1 - l)]
+    far_away_src = [dev(h2, c, z, x, l), dev(h2, 1 - c, z, x, l)]
     diag = jnp.logical_and(x == h, l == c)
     off_diag = jnp.logical_not(diag)
 
@@ -77,7 +81,7 @@
 
     others = [(dq, dc) for dq in range(NH) for dc in range(NC) if dq or dc]
     others_dev = [dev(x, l, z, add(h, dq, NH), add(c, dc, NC)) for dq, dc in others]
-    met = others_dev + [xp, xm, yl] + ring_z[1:] + [away_src]
+    met = others_dev + [xp, xm, yl] + ring_z[1:] + far + far_away_src + [away_src]
 
     @pl.when(off_diag)
     def _():
@@ -104,10 +108,19 @@
         sent.append(cp)
         return cp
 
+    loads = [
+        pltpu.make_async_copy(src, dst, lsem.at[i])
+        for i, (src, dst) in enumerate(
+            ((embt_in, embt), (hidt_in, hidt), (tgt_in, tgt), (pat_in, pat), (lgr_in, lgr))
+        )
+    ]
+    for cp in loads:
+        cp.start()
     piece[...] = jnp.zeros((PAD, TILE), BF)
+    loads[0].wait()
     piece[:PIECE] = embt[...]
     pl.semaphore_wait(bar, jnp.where(off_diag, len(met) + 1, len(met)))
-    swap = copy(piece, stage.at[z], turned)
+    swap = copy(piece, et.at[0, z], turned)
 
     @pl.when(off_diag)
     def _():
@@ -115,50 +128,72 @@
 
     @pl.when(diag)
     def _():
-        stage[z] = piece[...]
-
-    a, b = iotas((FEAT, NZ * PAD))
-    q = (b * 683) >> 16
-    sel[...] = mask_bf16(jnp.logical_and(b - PAD * q < PIECE, a == b - (PAD - PIECE) * q))
+        et[0, z] = piece[...]
+
+    for cp in loads[1:]:
+        cp.wait()
+    hidp[...] = jnp.zeros((NZ, PAD, TOK), BF)
+    for k in range(NZ):
+        hidp[k, :PIECE] = hidt[k * PIECE : (k + 1) * PIECE]
 
     @pl.when(off_diag)
     def _():
         swap.wait()
 
-    over_z = [send(stage.at[z], stage.at[z], ring_z[d]) for d in (4, 3, 5, 2, 6, 1, 7)]
-    a, b = iotas((TOK, TOK))
-    hid[...] = nt(mask_bf16(a == b), hidt[...]).astype(BF)
-    b, a = iotas((NZ * PAD, FEAT))
-    q = (b * 683) >> 16
-    selt[...] = mask_bf16(jnp.logical_and(b - PAD * q < PIECE, a == b - (PAD - PIECE) * q))
-    for cp in over_z:
-        cp.wait_recv()
-    et[0] = nn(sel[...], stage[...].reshape(NZ * PAD, TILE)).astype(BF)
-
-    rows2 = [pl.ds(0, HROW), pl.ds(HROW, HROW)]
-
-    def pass_on(src, dst, to, half):
-        return send(et.at[src, rows2[half]], et.at[dst, rows2[half]], to)
-
-    a1, a2, a3, b2, b3, c2, c3 = [], [], [], [], [], [], []
-    for half in range(2):
-        a1.append(pass_on(0, 1, yl, half))
-        a2.append(pass_on(0, 6, xp, half))
-        a3.append(pass_on(0, 2, xm, half))
-    for half in range(2):
-        a1[half].wait_recv()
-        b2.append(pass_on(1, 7, xp, half))
-        b3.append(pass_on(1, 3, xm, half))
-        a3[half].wait_recv()
-        c3.append(pass_on(2, 4, xm, half))
+
+    def over_z(slot):
+        own = et.at[slot, z]
+        return {d: send(own, own, ring_z[d]) for d in ORDER_Z}
+
+    z_own = over_z(0)
+    a1, a2, a3, b2, b3 = {}, {}, {}, {}, {}
+
+    def pass_on(src, dst, to, d):
+        k = add(z, d, NZ)
+        return send(et.at[src, k], et.at[dst, k], to)
+
+    def spread_own(d):
+        if d:
+            z_own[NZ - d].wait_recv()
+        a1[d] = pass_on(0, 1, yl, d)
+        a2[d] = pass_on(0, 6, xp, d)
+        a3[d] = pass_on(0, 2, xm, d)
+
+    def spread_yl(d):
+        a1[d].wait_recv()
+        b2[d] = pass_on(1, 7, xp, d)
+        b3[d] = pass_on(1, 3, xm, d)
+
+    spread_own(0)
+    far_in = [send(et.at[0, z], et.at[4 + m, z], far[m]) for m in range(2)]
+    spread_own(1)
+    spread_own(7)
+    spread_yl(0)
+    z_far = []
+    for m in range(2):
+        far_in[m].wait_recv()
+        z_far.append(over_z(4 + m))
+    spread_own(2)
+    spread_own(6)
+    spread_yl(1)
+    spread_yl(7)
+    spread_own(3)
+    spread_own(5)
+    spread_yl(2)
+    spread_yl(6)
+    spread_own(4)
+    spread_yl(3)
+    spread_yl(5)
+    spread_yl(4)
 
     def weights(r):
-        return jnp.concatenate([et[2 * r], et[2 * r + 1]], axis=1)
+        parts = [et[2 * r + m].reshape(NZ * PAD, TILE) for m in range(2)]
+        return jnp.concatenate(parts, axis=1)
 
     sib_cp, q_cp = {}, {}
 
     def logits(r):
-        s = nn(hid[...], weights(r))
+        s = tn(hidp[...].reshape(NZ * PAD, TOK), weights(r))
         base = lax.rem(x + r, NX) * 2
         _, lane = iotas((TILE, WIDE))
         block = base + jnp.where(lane < TILE, l, 1 - l)
@@ -196,21 +231,20 @@
         lsum[r] = total
 
     logits(0)
-    b2[0].wait_recv()
-    c2.append(pass_on(7, 5, xp, 0))
     spread(0)
-    b2[1].wait_recv()
-    c2.append(pass_on(7, 5, xp, 1))
-    for cp in b3:
-        cp.wait_recv()
+    for d in range(NZ):
+        a3[d].wait_recv()
+        b3[d].wait_recv()
     logits(1)
-    for cp in a2:
-        cp.wait_recv()
+    for d in range(NZ):
+        a2[d].wait_recv()
+        b2[d].wait_recv()
     logits(3)
     spread(1)
     spread(3)
-    for cp in c3 + c2:
-        cp.wait_recv()
+    for m in range(2):
+        for d in ORDER_Z:
+            z_far[m][d].wait_recv()
     logits(2)
     whole(0)
     spread(2)
@@ -239,7 +273,7 @@
     at_target = sum(jnp.where(hit, s, 0.0) for hit, s in zip(hits, ls))
     loss = lse - jnp.sum(at_target, axis=1, keepdims=True)
     g_cp, relay = {}, {}
-    for r in (2, 1, 3, 0):
+    for r in (1, 3, 2, 0):
         probs = jnp.exp(ls[r] - lse)
         gbuf[r, h, c] = (scale * (probs - jnp.where(hits[r], 1.0, 0.0))).astype(BF)
         own = gbuf.at[r, h, c]
@@ -258,63 +292,59 @@
         relay[r].wait_recv()
         return nn(hidt[...], gbuf[r].reshape(TOK, WIDE))
 
+    def to_near(r, to):
+        d = grad(r)
+        out = []
+        for m in range(2):
+            xo[r // 2, m] = d[:, m * TILE : (m + 1) * TILE].astype(BF)
+            out.append(send(xo.at[r // 2, m], xin.at[r // 2, m], to))
+        return out
+
+    def to_z(slot, tot):
+        for k in range(NZ):
+            pieces[slot, k, :PIECE] = tot[k * PIECE : (k + 1) * PIECE].astype(BF)
+        pin[slot, z] = pieces[slot, z]
+        return [send(pieces.at[slot, add(z, d, NZ)], pin.at[slot, z], ring_z[d]) for d in ORDER_Z]
+
+    def sum_z(slot, cps):
+        for cp in cps:
+            cp.wait_recv()
+        total = pin[slot, 0].astype(F32)
+        for k in range(1, NZ):
+            total = total + pin[slot, k].astype(F32)
+        zsum[slot] = total.astype(BF)
+
+    pieces[...] = jnp.zeros((4, NZ, PAD, TILE), BF)
+    pair(1)
+    near_p = to_near(1, xp)
+    pair(3)
+    near_m = to_near(3, xm)
     pair(2)
     d = grad(2)
-    xo[0] = d[:, :TILE].astype(BF)
-    far_p = send(xo.at[0], xin.at[0], xp)
-    xo[1] = d[:, TILE:].astype(BF)
-    far_m = send(xo.at[1], xin.at[1], xm)
-    pair(1)
-    d = grad(1)
-    xo[2] = d[:, TILE:].astype(BF)
-    p1 = send(xo.at[2], xin.at[2], xp)
-    tbuf[0] = d[:, :TILE]
-    pair(3)
-    d = grad(3)
-    xo[3] = d[:, :TILE].astype(BF)
-    m0 = send(xo.at[3], xin.at[3], xm)
-    tbuf[1] = d[:, TILE:]
+    z_cp = {2 + m: to_z(2 + m, d[:, m * TILE : (m + 1) * TILE]) for m in range(2)}
     pair(0)
-    far_p.wait_recv()
-    xs[0] = (tbuf[0] + xin[0].astype(F32)).astype(BF)
-    p0 = send(xs.at[0], xin.at[4], xp)
-    far_m.wait_recv()
-    xs[1] = (tbuf[1] + xin[1].astype(F32)).astype(BF)
-    m1 = send(xs.at[1], xin.at[5], xm)
-    d = grad(0)
-    tbuf[0] = d[:, :TILE]
-    tbuf[1] = d[:, TILE:]
+    own = grad(0)
+    for m in range(2):
+        near_p[m].wait_recv()
+        near_m[m].wait_recv()
+        near = xin[0, m].astype(F32) + xin[1, m].astype(F32)
+        z_cp[m] = to_z(m, own[:, m * TILE : (m + 1) * TILE] + near)
 
     hg = nt(weights(0), gbuf[0].reshape(TOK, WIDE))
     for r in range(1, NX):
         hg = hg + nt(weights(r), gbuf[r].reshape(TOK, WIDE))
-    hg_o[...] = hg.astype(BF)
+    for k in range(NZ):
+        hg_o[k * PIECE : (k + 1) * PIECE] = hg[k * PAD : k * PAD + PIECE].astype(BF)
     for cp in loss_cp:
         cp.wait_recv()
     for t in range(NH):
         loss_o[t : t + 1, :] = lbuf[2 * t, 0:1, :] + lbuf[2 * t + 1, 0:1, :]
 
-    z_cp = [[], []]
-    for m, (near, far) in ((1, (p1, m1)), (0, (m0, p0))):
-        near.wait_recv()
-        far.wait_recv()
-        tot = tbuf[m] + xin[(3, 2)[m]].astype(F32) + xin[(4, 5)[m]].astype(F32)
-        pieces[m] = nn(selt[...], tot.astype(BF)).astype(BF).reshape(NZ, PAD, TILE)
-        for d in (4, 3, 5, 2, 6, 1, 7):
-            z_cp[m].append(send(pieces.at[m, add(z, d, NZ)], pin.at[m, z], ring_z[d]))
-        pin[m, z] = pieces[m, z]
-
-    def over_z_sum(m):
-        for cp in z_cp[m]:
-            cp.wait_recv()
-        total = pin[m, 0].astype(F32)
-        for k in range(1, NZ):
-            total = total + pin[m, k].astype(F32)
-        zsum[m] = total.astype(BF)
-
-    over_z_sum(1)
-    end1 = send(zsum.at[1], fin.at[1], away)
-    over_z_sum(0)
+    end = {}
+    for slot in (2, 3):
+        sum_z(slot, z_cp[slot])
+        end[slot] = send(zsum.at[slot], fin.at[slot], far_away[slot - 2])
+    sum_z(0, z_cp[0])
     end0 = copy(zsum.at[0], fin.at[0], turned)
 
     @pl.when(off_diag)
@@ -325,13 +355,19 @@
     def _():
         fin[0] = zsum[0]
 
-    end1.wait_recv()
+    sum_z(1, z_cp[1])
+    end[1] = send(zsum.at[1], fin.at[1], away)
+    for cp in end.values():
+        cp.wait_recv()
 
     @pl.when(off_diag)
     def _():
         end0.wait()
 
-    eg_o[...] = (fin[0].astype(F32) + fin[1].astype(F32))[:PIECE]
+    total = fin[0].astype(F32)
+    for slot in range(1, 4):
+        total = total + fin[slot].astype(F32)
+    eg_o[...] = total[:PIECE]
     for cp in sent:
         cp.wait_send()
 
@@ -345,15 +381,17 @@
             jax.ShapeDtypeStruct((FEAT, TOK), BF),
             jax.ShapeDtypeStruct((PIECE, TILE), F32),
         ),
-        in_specs=[vmem] * 5,
+        in_specs=[pl.BlockSpec(memory_space=pltpu.HBM)] * 5,
         out_specs=(vmem,) * 3,
         scratch_shapes=[
+            pltpu.VMEM((FEAT, TOK), BF),
+            pltpu.VMEM((PIECE, TILE), BF),
+            pltpu.VMEM((NH, TILE), jnp.int32),
+            pltpu.VMEM((1, NH), jnp.int32),
+            pltpu.VMEM((NH, TILE), F32),
+            pltpu.VMEM((NZ, PAD, TOK), BF),
             pltpu.VMEM((PAD, TILE), BF),
-            pltpu.VMEM((NZ, PAD, TILE), BF),
-            pltpu.VMEM((FEAT, NZ * PAD), BF),
-            pltpu.VMEM((NZ * PAD, FEAT), BF),
-            pltpu.VMEM((TOK, FEAT), BF),
-            pltpu.VMEM((8, FEAT, TILE), BF),
+            pltpu.VMEM((8, NZ, PAD, TILE), BF),
             pltpu.VMEM((NX, NH, NC, HALF, WIDE), F32),
             pltpu.VMEM((NX, NH, HALF, WIDE), F32),
             pltpu.VMEM((NX, NH - 1, HALF, WIDE), I16),
@@ -363,16 +401,15 @@
             pltpu.VMEM((NX, HALF, WIDE), F32),
             pltpu.VMEM((NX, NH, NC, HALF, WIDE), BF),
             pltpu.VMEM((NH * NC, 8, TILE), F32),
-            pltpu.VMEM((4, FEAT, TILE), BF),
-            pltpu.VMEM((2, FEAT, TILE), BF),
-            pltpu.VMEM((6, FEAT, TILE), BF),
-            pltpu.VMEM((2, FEAT, TILE), F32),
-            pltpu.VMEM((2, NZ, PAD, TILE), BF),
-            pltpu.VMEM((2, NZ, PAD, TILE), BF),
-            pltpu.VMEM((2, PAD, TILE), BF),
-            pltpu.VMEM((2, PAD, TILE), BF),
+            pltpu.VMEM((2, 2, FEAT, TILE), BF),
+            pltpu.VMEM((2, 2, FEAT, TILE), BF),
+            pltpu.VMEM((4, NZ, PAD, TILE), BF),
+            pltpu.VMEM((4, NZ, PAD, TILE), BF),
+            pltpu.VMEM((4, PAD, TILE), BF),
+            pltpu.VMEM((4, PAD, TILE), BF),
             pltpu.SemaphoreType.DMA((NSEM,)),
             pltpu.SemaphoreType.DMA((NSEM,)),
+            pltpu.SemaphoreType.DMA((5,)),
         ],
         compiler_params=pltpu.CompilerParams(
             collective_id=0, has_side_effects=True, vmem_limit_bytes=48 << 20

time: 100 us -> 97.8 us (0.978); the launches traced: 98.2 us -> 97.6 us
  no operation moved by 1% of the time
where the time goes in v3:
time: 97.8 us; the launch traced here: 97.6 us
  Pallas kernels  92.4 us (94%)
  local copies, waits for them, and re-layouts  4.55 us (5%)
    pallas_call x1, Pallas kernels, on_device(): pl.pallas_call(kernel, out_shape=(jax.ShapeDtypeStruct((NH, TILE), F32),...  92.4 us
    unnamed x13, local copies, waits for them, and re-layouts  4.55 us

profile of v3, /device:TPU:7, one launch (start us, length us, event | category | flops | bytes accessed | tf_op | source)
XLA Modules:
  0.0 97.6 jit_solution(14079591993737666949)
XLA Ops:
  0.6 0.0 copy-start.3
  0.6 0.0 copy-start.2
  0.7 0.0 copy-start.4
  0.7 0.7 copy-done.3
  1.3 0.0 copy-done.2
  1.3 0.0 copy-done.4
  1.3 0.0 copy-start
  1.3 1.1 %copy-done = bf16[512,672]{0,1:T(8,128)(2,1)S(1)} copy-done((bf16[512,672]{0,1:T(8,128)(2,1)S(1)}, bf16[512,672]{0,1:T(8,128)(2,1)}, u32[]{:S(2)}) %copy-start) | copy-done | bytes 688152
  2.4 0.0 copy-start.1
  2.4 0.7 copy-done.1
  3.2 92.4 %shard_map.76 = (f32[4,128]{1,0:T(4,128)S(1)}, bf16[672,512]{1,0:T(8,128)(2,1)S(1)}, f32[84,128]{1,0:T(8,128)S(1)}) custom-call(bf16[672,512]{1,0:T(8,128)(2,1)S(1)} %bitcast.8, bf16[84,128]{1,0:T(8,128)(2,1)S(1)} %bitcast.11, s32[4,128]{1,0:T(4,128)S(1)} %bitcast.12, s32[1,4]{1,0:T(1,128)S(1)} %bitcast.15, f32[4,128]{1,0:T(4,128)S(1)} %bitcast.13), custom_call_target="tpu_custom_call" | custom-call | tf_op jit(solution)/shard_map/pallas_call | solution.py:377
  95.5 0.6 copy.11
  96.1 0.8 copy.12
  97.0 0.6 copy.13
Async XLA Ops:
  0.6 0.7 copy-start.3
  0.6 0.7 copy-start.2
  0.7 0.7 copy-start.4
  1.3 1.1 %copy-start = (bf16[512,672]{0,1:T(8,128)(2,1)S(1)}, bf16[512,672]{0,1:T(8,128)(2,1)}, u32[]{:S(2)}) copy-start(bf16[512,672]{0,1:T(8,128)(2,1)} %param.5) | copy-start | bytes 2064388
  2.4 0.7 copy-start.1

commit v4 on v3

v4 whole, which is shorter than its diff:
```python
import jax
import jax.numpy as jnp
from jax import lax
from jax.experimental import pallas as pl
from jax.experimental.pallas import tpu as pltpu
from jax.sharding import PartitionSpec as P

MESH = pl.DeviceIdType.MESH
BF = jnp.bfloat16
F32 = jnp.float32
I16 = jnp.int16
DEAD = -1e30
TOP = 32767.0
NX, NL, NZ, NH, NC = 4, 2, 8, 4, 2
TILE = 128
HALF = 64
WIDE = 2 * TILE
TOK = 512
FEAT = 672
PIECE = 84
PAD = 96
NSEM = 64
BLOCKS = ((0, 0), (0, 1), (1, 0), (3, 0), (1, 1), (3, 1), (2, 0), (2, 1))
ORDER_Z = (1, 7, 2, 6, 3, 5, 4)


def nt(a, b):
    return lax.dot_general(a, b, (((1,), (1,)), ((), ())), preferred_element_type=F32)


def tn(a, b):
    return lax.dot_general(a, b, (((0,), (0,)), ((), ())), preferred_element_type=F32)


def nn(a, b):
    return jnp.dot(a, b, preferred_element_type=F32)


def iotas(shape):
    return lax.broadcasted_iota(jnp.int32, shape, 0), lax.broadcasted_iota(jnp.int32, shape, 1)


def largest(a):
    return jnp.max(jnp.max(a, axis=1, keepdims=True), axis=0, keepdims=True)


def kernel(
    hidt, embt, tgt, pat, lgr, loss_o, hg_o, eg_o,
    hidp, piece, et, sbuf, sib, qout, qstep, qin, qin_step, lsum,
    gbuf, lbuf, xo, xin, pieces, pin, zsum, fin, ssem, rsem,
):
    x = lax.axis_index("dp")
    ctx = lax.axis_index("ctx")
    v = lax.axis_index("vocab")
    l, z = lax.div(ctx, NZ), lax.rem(ctx, NZ)
    h, c = lax.div(v, NC), lax.rem(v, NC)

    def dev(x, l, z, h, c):
        return (x, l * NZ + z, h * NC + c)

    def add(a, d, n):
        return lax.rem(a + d, n)

    sibling = dev(x, l, z, h, 1 - c)
    ring_h = [dev(x, l, z, add(h, dq, NH), c) for dq in range(NH)]
    xp, xm = dev(add(x, 1, NX), l, z, h, c), dev(add(x, 3, NX), l, z, h, c)
    yl = dev(x, 1 - l, z, h, c)
    ring_z = [dev(x, l, add(z, d, NZ), h, c) for d in range(NZ)]
    turned = dev(h, c, z, x, l)
    away, away_src = dev(h, c, z, x, 1 - l), dev(h, 1 - c, z, x, l)
    x2, h2 = add(x, 2, NX), add(h, 2, NX)
    far = [dev(x2, l, z, h, c), dev(x2, 1 - l, z, h, c)]
    far_away = [dev(h, c, z, x2, l), dev(h, c, z, x2, 1 - l)]
    far_away_src = [dev(h2, c, z, x, l), dev(h2, 1 - c, z, x, l)]
    diag = jnp.logical_and(x == h, l == c)
    off_diag = jnp.logical_not(diag)

    bar = pltpu.get_barrier_semaphore()

    def greet(who):
        pl.semaphore_signal(bar, inc=1, device_id=who, device_id_type=MESH)

    others = [(dq, dc) for dq in range(NH) for dc in range(NC) if dq or dc]
    others_dev = [dev(x, l, z, add(h, dq, NH), add(c, dc, NC)) for dq, dc in others]
    met = others_dev + [xp, xm, yl] + ring_z[1:] + far + far_away_src + [away_src]

    @pl.when(off_diag)
    def _():
        greet(turned)

    for who in met:
        greet(who)

    count = [0]
    sent = []

    def group():
        count[0] += 1
        return count[0] - 1

    def copy(src, dst, to, i):
        return pltpu.make_async_remote_copy(
            src_ref=src, dst_ref=dst, send_sem=ssem.at[i], recv_sem=rsem.at[i],
            device_id=to, device_id_type=MESH,
        )

    def wait_in(ref, i):
        copy(ref, ref, sibling, i).wait_recv()

    def wait_out(ref, i):
        copy(ref, ref, sibling, i).wait_send()

    def send_all(copies, ref):
        i = group()
        for src, dst, to in copies:
            copy(src, dst, to, i).start()
        sent.append((ref, i))
        return ref, i

    def send(src, dst, to):
        return send_all([(src, dst, to)], src)

    piece[...] = jnp.zeros((PAD, TILE), BF)
    piece[:PIECE] = embt[...]
    pl.semaphore_wait(bar, jnp.where(off_diag, len(met) + 1, len(met)))
    swap = copy(piece, et.at[0, z], turned, group())

    @pl.when(off_diag)
    def _():
        swap.start()

    @pl.when(diag)
    def _():
        et[0, z] = piece[...]

    hidp[...] = jnp.zeros((NZ, PAD, TOK), BF)
    for k in range(NZ):
        hidp[k, :PIECE] = hidt[k * PIECE : (k + 1) * PIECE]

    @pl.when(off_diag)
    def _():
        swap.wait()


    def index(d):
        return add(z, d, NZ)

    z_own = {d: send(et.at[0, z], et.at[0, z], ring_z[d]) for d in ORDER_Z}
    a1, groups = {}, [group() for _ in range(4)]

    def pass_on(src, dst, to, d, i):
        copy(et.at[src, index(d)], et.at[dst, index(d)], to, i).start()

    def spread_own(d):
        if d:
            wait_in(*z_own[NZ - d])
        part = et.at[0, index(d)]
        a1[d] = send(part, et.at[1, index(d)], yl)
        pass_on(0, 3, xp, d, groups[0])
        pass_on(0, 2, xm, d, groups[1])

    def spread_yl(d):
        wait_in(*a1[d])
        pass_on(1, 5, xp, d, groups[2])
        pass_on(1, 4, xm, d, groups[3])

    spread_own(0)
    far_in = [send(et.at[0, z], et.at[6 + m, z], far[m]) for m in range(2)]
    spread_own(1)
    spread_own(7)
    spread_yl(0)
    z_far = []
    for m in range(2):
        wait_in(*far_in[m])
        part = et.at[6 + m, z]
        copies = [(part, part, ring_z[d]) for d in ORDER_Z]
        z_far.append(send_all(copies, et.at[6 + m, pl.ds(0, NZ - 1)]))
    spread_own(2)
    spread_own(6)
    spread_yl(1)
    spread_yl(7)
    spread_own(3)
    spread_own(5)
    spread_yl(2)
    spread_yl(6)
    spread_own(4)
    spread_yl(3)
    spread_yl(5)
    spread_yl(4)
    for k, slot in enumerate((3, 2, 5, 4)):
        sent.append((et.at[slot], groups[k]))

    def weights(r):
        parts = [et[2 * r + m].reshape(NZ * PAD, TILE) for m in range(2)]
        return jnp.concatenate(parts, axis=1)

    def block_of(slot):
        dx, m = BLOCKS[slot]
        return 2 * add(x, dx, NX) + (1 - l if m else l)

    sib_cp, q_cp = {}, {}

    def logits(r):
        s = tn(hidp[...].reshape(NZ * PAD, TOK), weights(r))
        _, lane = iotas((TILE, WIDE))
        block = jnp.where(lane < TILE, block_of(2 * r), block_of(2 * r + 1))
        for t in range(NH):
            off = jnp.logical_and(block == v, pat[0:1, t : t + 1] == 0)
            part = jnp.where(off, DEAD, s[t * TILE : (t + 1) * TILE])
            sbuf[r, t] = part.reshape(NC, HALF, WIDE)
        sib_cp[r] = send(sbuf.at[r, :, 1 - c], sib.at[r], sibling)

    def mine(r, dq):
        t = add(h, dq, NH)
        return sbuf[r, t, c] + sib[r, t]

    def spread(r):
        wait_in(*sib_cp[r])
        tiles, steps = [], []
        for dq in (2, 1, 3):
            s = mine(r, dq)
            dead = s < 0.5 * DEAD
            peak = largest(jnp.where(dead, 0.0, jnp.abs(s)))
            step = jnp.maximum(peak, 1e-30) * (1.0 / TOP)
            near = jnp.clip(jnp.round(s * (1.0 / step)), -TOP, TOP)
            qout[r, dq - 1] = jnp.where(dead, -TOP - 1.0, near).astype(jnp.int32).astype(I16)
            qstep[r, dq - 1] = jnp.broadcast_to(step, (8, TILE))
            tiles.append((qout.at[r, dq - 1], qin.at[r, dq - 1], ring_h[dq]))
            steps.append((qstep.at[r, dq - 1], qin_step.at[r, dq - 1], ring_h[dq]))
        q_cp[r] = (send_all(steps, qstep.at[r]), send_all(tiles, qout.at[r]))

    def whole(r):
        total = mine(r, 0)
        for cp in q_cp[r]:
            wait_in(*cp)
        for k in range(NH - 1):
            steps = qin[r, k].astype(jnp.int32).astype(F32)
            total = total + jnp.where(steps < -TOP - 0.5, DEAD, steps * qin_step[r, k, 0:1, 0:1])
        lsum[r] = total

    logits(0)
    spread(0)
    wait_in(et.at[2], groups[1])
    wait_in(et.at[3], groups[0])
    logits(1)
    wait_in(et.at[4], groups[3])
    wait_in(et.at[5], groups[2])
    logits(2)
    spread(1)
    spread(2)
    for m in range(2):
        wait_in(*z_far[m])
    logits(3)
    whole(0)
    spread(3)
    whole(1)
    whole(2)
    whole(3)

    sub, lane = iotas((HALF, TILE))
    turn = sub + c * HALF == lane

    def column(row):
        return jnp.sum(jnp.where(turn, row, 0.0), axis=1, keepdims=True)

    target = column(tgt[pl.ds(h, 1), :].astype(F32)).astype(jnp.int32)
    scale = column(lgr[pl.ds(h, 1), :])
    _, lane2 = iotas((HALF, WIDE))
    hits, ls = [], []
    for r in range(NX):
        col = jnp.where(lane2 < TILE, block_of(2 * r), block_of(2 * r + 1) - 1) * TILE + lane2
        hits.append(col == target)
        ls.append(lsum[r])
    peak = jnp.maximum(jnp.maximum(ls[0], ls[1]), jnp.maximum(ls[2], ls[3]))
    peak = jnp.max(peak, axis=1, keepdims=True)
    total = jnp.sum(sum(jnp.exp(s - peak) for s in ls), axis=1, keepdims=True)
    lse = peak + jnp.log(total)
    at_target = sum(jnp.where(hit, s, 0.0) for hit, s in zip(hits, ls))
    loss = lse - jnp.sum(at_target, axis=1, keepdims=True)
    g_cp, relay = {}, {}
    for r in (3, 1, 2, 0):
        probs = jnp.exp(ls[r] - lse)
        gbuf[r, h, c] = (scale * (probs - jnp.where(hits[r], 1.0, 0.0))).astype(BF)
        own = gbuf.at[r, h, c]
        copies = [(own, own, ring_h[dq]) for dq in (2, 1, 3)]
        g_cp[r] = send_all(copies, gbuf.at[r, pl.ds(0, NH - 1), 0])
    loss_row = jnp.sum(jnp.where(turn, loss, 0.0), axis=0, keepdims=True)
    lbuf[v] = jnp.broadcast_to(loss_row, (8, TILE))
    copies = [(lbuf.at[v], lbuf.at[v], who) for who in others_dev]
    loss_cp = send_all(copies, lbuf.at[pl.ds(0, NH * NC - 1)])

    def pair(r):
        wait_in(*g_cp[r])
        part = gbuf.at[r, :, c]
        relay[r] = send(part, part, sibling)

    def grad(r):
        wait_in(*relay[r])
        return nn(hidt[...], gbuf[r].reshape(TOK, WIDE))

    def to_near(m):
        d = grad(1 + m)
        out = []
        for side, to in enumerate((xp, xm)):
            xo[side, m] = d[:, side * TILE : (side + 1) * TILE].astype(BF)
            out.append(send(xo.at[side, m], xin.at[side, m], to))
        return out

    def to_z(slot, tot):
        for k in range(NZ):
            pieces[slot, k, :PIECE] = tot[k * PIECE : (k + 1) * PIECE].astype(BF)
        pin[slot, z] = pieces[slot, z]
        copies = [(pieces.at[slot, index(d)], pin.at[slot, z], ring_z[d]) for d in ORDER_Z]
        return send_all(copies, pieces.at[slot, pl.ds(0, NZ - 1)])

    def sum_z(slot):
        wait_in(*z_cp[slot])
        total = pin[slot, 0].astype(F32)
        for k in range(1, NZ):
            total = total + pin[slot, k].astype(F32)
        zsum[slot] = total.astype(BF)

    pieces[...] = jnp.zeros((4, NZ, PAD, TILE), BF)
    pair(3)
    d = grad(3)
    z_cp = {2 + m: to_z(2 + m, d[:, m * TILE : (m + 1) * TILE]) for m in range(2)}
    pair(1)
    near = [to_near(0)]
    pair(2)
    near.append(to_near(1))
    pair(0)
    own = grad(0)
    for m in range(2):
        for cp in near[m]:
            wait_in(*cp)
        both = xin[0, m].astype(F32) + xin[1, m].astype(F32)
        z_cp[m] = to_z(m, own[:, m * TILE : (m + 1) * TILE] + both)

    hg = nt(weights(0), gbuf[0].reshape(TOK, WIDE))
    for r in range(1, NX):
        hg = hg + nt(weights(r), gbuf[r].reshape(TOK, WIDE))
    for k in range(NZ):
        hg_o[k * PIECE : (k + 1) * PIECE] = hg[k * PAD : k * PAD + PIECE].astype(BF)
    wait_in(*loss_cp)
    for t in range(NH):
        loss_o[t : t + 1, :] = lbuf[2 * t, 0:1, :] + lbuf[2 * t + 1, 0:1, :]

    end = []
    for slot in (2, 3):
        sum_z(slot)
        end.append(send(zsum.at[slot], fin.at[slot], far_away[slot - 2]))
    sum_z(0)
    end0 = copy(zsum.at[0], fin.at[0], turned, group())

    @pl.when(off_diag)
    def _():
        end0.start()

    @pl.when(diag)
    def _():
        fin[0] = zsum[0]

    sum_z(1)
    end.append(send(zsum.at[1], fin.at[1], away))
    for cp in end:
        wait_in(*cp)

    @pl.when(off_diag)
    def _():
        end0.wait()

    total = fin[0].astype(F32)
    for slot in range(1, 4):
        total = total + fin[slot].astype(F32)
    eg_o[...] = total[:PIECE]
    for cp in sent:
        wait_out(*cp)


def on_device(hidden, embedding, targets, pattern, loss_grad):
    vmem = pl.BlockSpec(memory_space=pltpu.VMEM)
    loss, hidden_grad, embedding_grad = pl.pallas_call(
        kernel,
        out_shape=(
            jax.ShapeDtypeStruct((NH, TILE), F32),
            jax.ShapeDtypeStruct((FEAT, TOK), BF),
            jax.ShapeDtypeStruct((PIECE, TILE), F32),
        ),
        in_specs=[vmem] * 5,
        out_specs=(vmem,) * 3,
        scratch_shapes=[
            pltpu.VMEM((NZ, PAD, TOK), BF),
            pltpu.VMEM((PAD, TILE), BF),
            pltpu.VMEM((8, NZ, PAD, TILE), BF),
            pltpu.VMEM((NX, NH, NC, HALF, WIDE), F32),
            pltpu.VMEM((NX, NH, HALF, WIDE), F32),
            pltpu.VMEM((NX, NH - 1, HALF, WIDE), I16),
            pltpu.VMEM((NX, NH - 1, 8, TILE), F32),
            pltpu.VMEM((NX, NH - 1, HALF, WIDE), I16),
            pltpu.VMEM((NX, NH - 1, 8, TILE), F32),
            pltpu.VMEM((NX, HALF, WIDE), F32),
            pltpu.VMEM((NX, NH, NC, HALF, WIDE), BF),
            pltpu.VMEM((NH * NC, 8, TILE), F32),
            pltpu.VMEM((2, 2, FEAT, TILE), BF),
            pltpu.VMEM((2, 2, FEAT, TILE), BF),
            pltpu.VMEM((4, NZ, PAD, TILE), BF),
            pltpu.VMEM((4, NZ, PAD, TILE), BF),
            pltpu.VMEM((4, PAD, TILE), BF),
            pltpu.VMEM((4, PAD, TILE), BF),
            pltpu.SemaphoreType.DMA((NSEM,)),
            pltpu.SemaphoreType.DMA((NSEM,)),
        ],
        compiler_params=pltpu.CompilerParams(
            collective_id=0, has_side_effects=True, vmem_limit_bytes=48 << 20
        ),
    )(hidden.T, embedding.T, targets.reshape(NH, TILE), pattern.T, loss_grad.reshape(NH, TILE))
    return loss.reshape(TOK), hidden_grad.T, embedding_grad.T


def solution(mesh):
    return jax.shard_map(
        on_device,
        mesh=mesh,
        in_specs=(
            P(("dp", "ctx"), "vocab"),
            P("vocab", ("dp", "ctx")),
            P(("dp", "ctx")),
            P(("dp", "ctx"), "vocab"),
            P(("dp", "ctx")),
        ),
        out_specs=(P(("dp", "ctx")), P(("dp", "ctx"), "vocab"), P("vocab", ("dp", "ctx"))),
        check_vma=False,
    )
```

time: 97.8 us -> 91.8 us (0.939)
  Pallas kernels: 92.4 us -> 85.5 us
    pallas_call x1, Pallas kernels: 92.4 us -> 85.5 us  [on_device(): pl.pallas_call(kernel, out_shape=(jax.ShapeDtypeStruct((NH, TILE), F32),...]
where the time goes in v4:
time: 91.8 us; the launch traced here: 90.7 us
  Pallas kernels  85.5 us (93%)
  local copies, waits for them, and re-layouts  4.55 us (5%)
    pallas_call x1, Pallas kernels, on_device(): pl.pallas_call(kernel, out_shape=(jax.ShapeDtypeStruct((NH, TILE), F32),...  85.5 us
    unnamed x13, local copies, waits for them, and re-layouts  4.55 us

profile of v4, /device:TPU:7, one launch (start us, length us, event | category | flops | bytes accessed | tf_op | source)
XLA Modules:
  0.0 90.7 jit_solution(8583613391078246907)
XLA Ops:
  0.6 0.0 copy-start.3
  0.6 0.0 copy-start.2
  0.7 0.0 copy-start.4
  0.7 0.7 copy-done.3
  1.3 0.0 copy-done.2
  1.3 0.0 copy-done.4
  1.3 0.0 copy-start
  1.3 1.1 %copy-done = bf16[512,672]{0,1:T(8,128)(2,1)S(1)} copy-done((bf16[512,672]{0,1:T(8,128)(2,1)S(1)}, bf16[512,672]{0,1:T(8,128)(2,1)}, u32[]{:S(2)}) %copy-start) | copy-done | bytes 688152
  2.4 0.0 copy-start.1
  2.4 0.7 copy-done.1
  3.2 85.5 %shard_map.76 = (f32[4,128]{1,0:T(4,128)S(1)}, bf16[672,512]{1,0:T(8,128)(2,1)S(1)}, f32[84,128]{1,0:T(8,128)S(1)}) custom-call(bf16[672,512]{1,0:T(8,128)(2,1)S(1)} %bitcast.8, bf16[84,128]{1,0:T(8,128)(2,1)S(1)} %bitcast.11, s32[4,128]{1,0:T(4,128)S(1)} %bitcast.12, s32[1,4]{1,0:T(1,128)S(1)} %bitcast.15, f32[4,128]{1,0:T(4,128)S(1)} %bitcast.13), custom_call_target="tpu_custom_call" | custom-call | tf_op jit(solution)/shard_map/pallas_call | solution.py:382
  88.7 0.6 copy.11
  89.3 0.8 copy.12
  90.1 0.6 copy.13
Async XLA Ops:
  0.6 0.7 copy-start.3
  0.6 0.7 copy-start.2
  0.7 0.7 copy-start.4
  1.3 1.1 %copy-start = (bf16[512,672]{0,1:T(8,128)(2,1)S(1)}, bf16[512,672]{0,1:T(8,128)(2,1)}, u32[]{:S(2)}) copy-start(bf16[512,672]{0,1:T(8,128)(2,1)} %param.5) | copy-start | bytes 2064388
  2.4 0.7 copy-start.1

commit v5 on v4

--- a/solution.py
+++ b/solution.py
@@ -19,7 +19,7 @@
 FEAT = 672
 PIECE = 84
 PAD = 96
-NSEM = 64
+NSEM = 57
 BLOCKS = ((0, 0), (0, 1), (1, 0), (3, 0), (1, 1), (3, 1), (2, 0), (2, 1))
 ORDER_Z = (1, 7, 2, 6, 3, 5, 4)
 
@@ -224,7 +224,7 @@
             step = jnp.maximum(peak, 1e-30) * (1.0 / TOP)
             near = jnp.clip(jnp.round(s * (1.0 / step)), -TOP, TOP)
             qout[r, dq - 1] = jnp.where(dead, -TOP - 1.0, near).astype(jnp.int32).astype(I16)
-            qstep[r, dq - 1] = jnp.broadcast_to(step, (8, TILE))
+            qstep[r, dq - 1] = jnp.broadcast_to(step, (1, TILE))
             tiles.append((qout.at[r, dq - 1], qin.at[r, dq - 1], ring_h[dq]))
             steps.append((qstep.at[r, dq - 1], qin_step.at[r, dq - 1], ring_h[dq]))
         q_cp[r] = (send_all(steps, qstep.at[r]), send_all(tiles, qout.at[r]))
@@ -284,8 +284,7 @@
         own = gbuf.at[r, h, c]
         copies = [(own, own, ring_h[dq]) for dq in (2, 1, 3)]
         g_cp[r] = send_all(copies, gbuf.at[r, pl.ds(0, NH - 1), 0])
-    loss_row = jnp.sum(jnp.where(turn, loss, 0.0), axis=0, keepdims=True)
-    lbuf[v] = jnp.broadcast_to(loss_row, (8, TILE))
+    lbuf[v] = jnp.sum(jnp.where(turn, loss, 0.0), axis=0, keepdims=True)
     copies = [(lbuf.at[v], lbuf.at[v], who) for who in others_dev]
     loss_cp = send_all(copies, lbuf.at[pl.ds(0, NH * NC - 1)])
 
@@ -343,7 +342,7 @@
         hg_o[k * PIECE : (k + 1) * PIECE] = hg[k * PAD : k * PAD + PIECE].astype(BF)
     wait_in(*loss_cp)
     for t in range(NH):
-        loss_o[t : t + 1, :] = lbuf[2 * t, 0:1, :] + lbuf[2 * t + 1, 0:1, :]
+        loss_o[t : t + 1, :] = lbuf[2 * t] + lbuf[2 * t + 1]
 
     end = []
     for slot in (2, 3):
@@ -395,12 +394,12 @@
             pltpu.VMEM((NX, NH, NC, HALF, WIDE), F32),
             pltpu.VMEM((NX, NH, HALF, WIDE), F32),
             pltpu.VMEM((NX, NH - 1, HALF, WIDE), I16),
-            pltpu.VMEM((NX, NH - 1, 8, TILE), F32),
+            pltpu.VMEM((NX, NH - 1, 1, TILE), F32),
             pltpu.VMEM((NX, NH - 1, HALF, WIDE), I16),
-            pltpu.VMEM((NX, NH - 1, 8, TILE), F32),
+            pltpu.VMEM((NX, NH - 1, 1, TILE), F32),
             pltpu.VMEM((NX, HALF, WIDE), F32),
             pltpu.VMEM((NX, NH, NC, HALF, WIDE), BF),
-            pltpu.VMEM((NH * NC, 8, TILE), F32),
+            pltpu.VMEM((NH * NC, 1, TILE), F32),
             pltpu.VMEM((2, 2, FEAT, TILE), BF),
             pltpu.VMEM((2, 2, FEAT, TILE), BF),
             pltpu.VMEM((4, NZ, PAD, TILE), BF),

time: 91.8 us -> 89.9 us (0.979)
  the two profiles are of different devices: /device:TPU:7 before, /device:TPU:5 now
where the time goes in v5:
time: 89.9 us; the launch traced here: 89.7 us
  Pallas kernels  84.4 us (94%)
  local copies, waits for them, and re-layouts  4.55 us (5%)
    pallas_call x1, Pallas kernels, on_device(): pl.pallas_call(kernel, out_shape=(jax.ShapeDtypeStruct((NH, TILE), F32),...  84.4 us
    unnamed x13, local copies, waits for them, and re-layouts  4.55 us

profile of v5, /device:TPU:5, one launch (start us, length us, event | category | flops | bytes accessed | tf_op | source)
XLA Modules:
  0.0 89.7 jit_solution(15497244689815345193)
XLA Ops:
  0.6 0.0 copy-start.3
  0.6 0.0 copy-start.2
  0.7 0.0 copy-start.4
  0.7 0.7 copy-done.3
  1.3 0.0 copy-done.2
  1.3 0.0 copy-done.4
  1.3 0.0 copy-start
  1.3 1.1 %copy-done = bf16[512,672]{0,1:T(8,128)(2,1)S(1)} copy-done((bf16[512,672]{0,1:T(8,128)(2,1)S(1)}, bf16[512,672]{0,1:T(8,128)(2,1)}, u32[]{:S(2)}) %copy-start) | copy-done | bytes 688152
  2.4 0.0 copy-start.1
  2.4 0.7 copy-done.1
  3.2 84.4 %shard_map.76 = (f32[4,128]{1,0:T(4,128)S(1)}, bf16[672,512]{1,0:T(8,128)(2,1)S(1)}, f32[84,128]{1,0:T(8,128)S(1)}) custom-call(bf16[672,512]{1,0:T(8,128)(2,1)S(1)} %bitcast.8, bf16[84,128]{1,0:T(8,128)(2,1)S(1)} %bitcast.11, s32[4,128]{1,0:T(4,128)S(1)} %bitcast.12, s32[1,4]{1,0:T(1,128)S(1)} %bitcast.15, f32[4,128]{1,0:T(4,128)S(1)} %bitcast.13), custom_call_target="tpu_custom_call" | custom-call | tf_op jit(solution)/shard_map/pallas_call | solution.py:381
  87.6 0.6 copy.11
  88.2 0.8 copy.12
  89.0 0.6 copy.13
Async XLA Ops:
  0.6 0.7 copy-start.3
  0.6 0.7 copy-start.2
  0.7 0.7 copy-start.4
  1.3 1.1 %copy-start = (bf16[512,672]{0,1:T(8,128)(2,1)S(1)}, bf16[512,672]{0,1:T(8,128)(2,1)}, u32[]{:S(2)}) copy-start(bf16[512,672]{0,1:T(8,128)(2,1)} %param.5) | copy-start | bytes 2064388
  2.4 0.7 copy-start.1

commit v6 on v5

--- a/solution.py
+++ b/solution.py
@@ -47,7 +47,7 @@
 def kernel(
     hidt, embt, tgt, pat, lgr, loss_o, hg_o, eg_o,
     hidp, piece, et, sbuf, sib, qout, qstep, qin, qin_step, lsum,
-    gbuf, lbuf, xo, xin, pieces, pin, zsum, fin, ssem, rsem,
+    gbuf, lbuf, xo, xin, xfar, xfar_in, pieces, pin, zsum, fin, ssem, rsem,
 ):
     x = lax.axis_index("dp")
     ctx = lax.axis_index("ctx")
@@ -70,8 +70,7 @@
     away, away_src = dev(h, c, z, x, 1 - l), dev(h, 1 - c, z, x, l)
     x2, h2 = add(x, 2, NX), add(h, 2, NX)
     far = [dev(x2, l, z, h, c), dev(x2, 1 - l, z, h, c)]
-    far_away = [dev(h, c, z, x2, l), dev(h, c, z, x2, 1 - l)]
-    far_away_src = [dev(h2, c, z, x, l), dev(h2, 1 - c, z, x, l)]
+    far_away, far_away_src = dev(h, c, z, x2, l), dev(h2, c, z, x, l)
     diag = jnp.logical_and(x == h, l == c)
     off_diag = jnp.logical_not(diag)
 
@@ -82,7 +81,7 @@
 
     others = [(dq, dc) for dq in range(NH) for dc in range(NC) if dq or dc]
     others_dev = [dev(x, l, z, add(h, dq, NH), add(c, dc, NC)) for dq, dc in others]
-    met = others_dev + [xp, xm, yl] + ring_z[1:] + far + far_away_src + [away_src]
+    met = others_dev + [xp, xm, yl] + ring_z[1:] + far + [far_away_src, away_src]
 
     @pl.when(off_diag)
     def _():
@@ -301,7 +300,14 @@
         d = grad(1 + m)
         out = []
         for side, to in enumerate((xp, xm)):
-            xo[side, m] = d[:, side * TILE : (side + 1) * TILE].astype(BF)
+            part = d[:, side * TILE : (side + 1) * TILE]
+            if m:
+                wait_in(*far_x[side])
+                passing = xfar_in[side].astype(F32)
+                halves = [part[: FEAT // 2], part[FEAT // 2 :]]
+                halves[side] = halves[side] + passing
+                part = jnp.concatenate(halves, axis=0)
+            xo[side, m] = part.astype(BF)
             out.append(send(xo.at[side, m], xin.at[side, m], to))
         return out
 
@@ -309,7 +315,7 @@
         for k in range(NZ):
             pieces[slot, k, :PIECE] = tot[k * PIECE : (k + 1) * PIECE].astype(BF)
         pin[slot, z] = pieces[slot, z]
-        copies = [(pieces.at[slot, index(d)], pin.at[slot, z], ring_z[d]) for d in ORDER_Z]
+        copies = [(pieces.at[slot, index(d)], pin.at[slot, z], ring_z[d]) for d in (4, 3, 5, 2, 6, 1, 7)]
         return send_all(copies, pieces.at[slot, pl.ds(0, NZ - 1)])
 
     def sum_z(slot):
@@ -322,7 +328,12 @@
     pieces[...] = jnp.zeros((4, NZ, PAD, TILE), BF)
     pair(3)
     d = grad(3)
-    z_cp = {2 + m: to_z(2 + m, d[:, m * TILE : (m + 1) * TILE]) for m in range(2)}
+    far_x = []
+    for side, to in enumerate((xp, xm)):
+        rows = slice(side * FEAT // 2, (side + 1) * FEAT // 2)
+        xfar[side] = d[rows, TILE:].astype(BF)
+        far_x.append(send(xfar.at[side], xfar_in.at[side], to))
+    z_cp = {2: to_z(2, d[:, :TILE])}
     pair(1)
     near = [to_near(0)]
     pair(2)
@@ -345,9 +356,8 @@
         loss_o[t : t + 1, :] = lbuf[2 * t] + lbuf[2 * t + 1]
 
     end = []
-    for slot in (2, 3):
-        sum_z(slot)
-        end.append(send(zsum.at[slot], fin.at[slot], far_away[slot - 2]))
+    sum_z(2)
+    end.append(send(zsum.at[2], fin.at[2], far_away))
     sum_z(0)
     end0 = copy(zsum.at[0], fin.at[0], turned, group())
 
@@ -369,7 +379,7 @@
         end0.wait()
 
     total = fin[0].astype(F32)
-    for slot in range(1, 4):
+    for slot in range(1, 3):
         total = total + fin[slot].astype(F32)
     eg_o[...] = total[:PIECE]
     for cp in sent:
@@ -402,6 +412,8 @@
             pltpu.VMEM((NH * NC, 1, TILE), F32),
             pltpu.VMEM((2, 2, FEAT, TILE), BF),
             pltpu.VMEM((2, 2, FEAT, TILE), BF),
+            pltpu.VMEM((2, FEAT // 2, TILE), BF),
+            pltpu.VMEM((2, FEAT // 2, TILE), BF),
             pltpu.VMEM((4, NZ, PAD, TILE), BF),
             pltpu.VMEM((4, NZ, PAD, TILE), BF),
             pltpu.VMEM((4, PAD, TILE), BF),

time: 89.9 us -> 88.3 us (0.982)
  the two profiles are of different devices: /device:TPU:5 before, /device:TPU:7 now
where the time goes in v6:
time: 88.3 us; the launch traced here: 87.8 us
  Pallas kernels  82.6 us (94%)
  local copies, waits for them, and re-layouts  4.55 us (5%)
    pallas_call x1, Pallas kernels, on_device(): pl.pallas_call(kernel, out_shape=(jax.ShapeDtypeStruct((NH, TILE), F32),...  82.6 us
    unnamed x13, local copies, waits for them, and re-layouts  4.55 us

profile of v6, /device:TPU:7, one launch (start us, length us, event | category | flops | bytes accessed | tf_op | source)
XLA Modules:
  0.0 87.8 jit_solution(235187038467219408)
XLA Ops:
  0.6 0.0 copy-start.3
  0.6 0.0 copy-start.2
  0.7 0.0 copy-start.4
  0.7 0.7 copy-done.3
  1.3 0.0 copy-done.2
  1.3 0.0 copy-done.4
  1.3 0.0 copy-start
  1.3 1.1 %copy-done = bf16[512,672]{0,1:T(8,128)(2,1)S(1)} copy-done((bf16[512,672]{0,1:T(8,128)(2,1)S(1)}, bf16[512,672]{0,1:T(8,128)(2,1)}, u32[]{:S(2)}) %copy-start) | copy-done | bytes 688152
  2.4 0.0 copy-start.1
  2.4 0.7 copy-done.1
  3.2 82.6 %shard_map.76 = (f32[4,128]{1,0:T(4,128)S(1)}, bf16[672,512]{1,0:T(8,128)(2,1)S(1)}, f32[84,128]{1,0:T(8,128)S(1)}) custom-call(bf16[672,512]{1,0:T(8,128)(2,1)S(1)} %bitcast.8, bf16[84,128]{1,0:T(8,128)(2,1)S(1)} %bitcast.11, s32[4,128]{1,0:T(4,128)S(1)} %bitcast.12, s32[1,4]{1,0:T(1,128)S(1)} %bitcast.15, f32[4,128]{1,0:T(4,128)S(1)} %bitcast.13), custom_call_target="tpu_custom_call" | custom-call | tf_op jit(solution)/shard_map/pallas_call | solution.py:391
  85.7 0.6 copy.11
  86.3 0.8 copy.12
  87.2 0.6 copy.13
Async XLA Ops:
  0.6 0.7 copy-start.3
  0.6 0.7 copy-start.2
  0.7 0.7 copy-start.4
  1.3 1.1 %copy-start = (bf16[512,672]{0,1:T(8,128)(2,1)S(1)}, bf16[512,672]{0,1:T(8,128)(2,1)}, u32[]{:S(2)}) copy-start(bf16[512,672]{0,1:T(8,128)(2,1)} %param.5) | copy-start | bytes 2064388
  2.4 0.7 copy-start.1
